TPU v7x, 128 devices: a whole 4x4x4 slice. The times are simulated.
128 devices in a mesh: rows: 8 (over x, core), cols: 16 (over y, z).
Axes of the slice: x: 4, y: 4, z: 4, core: 2. Of those that a mesh axis runs over, the one named last changes fastest.
Arguments:
- grad: float32 [7168, 4096], P('rows', 'cols'), may hold values from -40 to 40
- basis: float32 [7168, 7168], P('rows', 'cols'), may hold values from -0.0625 to 0.0625
- mom_rot: float32 [7168, 4096], P('cols', 'rows'), may hold values from -6 to 6
- var_rot: float32 [7168, 4096], P('cols', 'rows'), may hold values from 0.25 to 4
- mom_plain: float32 [7168, 4096], P('rows', 'cols'), may hold values from -6 to 6
- var_plain: float32 [7168, 4096], P('rows', 'cols'), may hold values from 0.25 to 4
Outputs:
- update: float32 [7168, 4096], P('rows', 'cols')
- new_mom_rot: float32 [7168, 4096], P('cols', 'rows')
- new_var_rot: float32 [7168, 4096], P('cols', 'rows')
- new_mom_plain: float32 [7168, 4096], P('rows', 'cols')
- new_var_plain: float32 [7168, 4096], P('rows', 'cols')
All inputs are finite; a program needn't handle non-finite values.
Results may differ from a plain program's by a relative error of at most 0.00007.
Values sent between devices are 32-bit elements; how exact they have to be, the bound alone decides.
A program may use at most 128 MiB of HBM per device.

v0:
```python
import jax
import jax.numpy as jnp
from jax import lax
from jax.sharding import PartitionSpec as P

STEP = 10


beta_one = 0.95
beta_two = 0.95
eps_adam = 1e-08


def adam_step(moment, second, values):
    moment_new = beta_one * moment + (1.0 - beta_one) * values
    second_new = beta_two * second + (1.0 - beta_two) * values * values
    corr_one = 1.0 - beta_one**STEP
    corr_two = 1.0 - beta_two**STEP
    step_dir = moment_new / corr_one / (jnp.sqrt(second_new / corr_two) + eps_adam)
    return (moment_new, second_new, step_dir)


def per_device(grad, basis, mom_rot, var_rot, mom_plain, var_plain):
    new_mom_plain, new_var_plain, plain = adam_step(mom_plain, var_plain, grad)
    plain_local = jnp.sum(plain * plain)
    graft_total = lax.psum(plain_local, ("rows", "cols"))
    partial_rot = lax.dot_general(
        basis,
        lax.all_gather(grad, "cols", axis=1, tiled=True),
        (((0,), (0,)), ((), ())),
        precision=lax.Precision.HIGHEST,
        preferred_element_type=jnp.float32,
    )
    rotated = lax.psum_scatter(partial_rot, "rows", scatter_dimension=1, tiled=True)
    new_mom_rot, new_var_rot, direction = adam_step(mom_rot, var_rot, rotated)
    partial_back = jnp.dot(
        basis,
        lax.all_gather(direction, "rows", axis=1, tiled=True),
        precision=lax.Precision.HIGHEST,
        preferred_element_type=jnp.float32,
    )
    back = lax.psum_scatter(partial_back, "cols", scatter_dimension=1, tiled=True)
    back_local = jnp.sum(back * back)
    own_total = lax.psum(back_local, ("rows", "cols"))
    update = back * (jnp.sqrt(graft_total) / (jnp.sqrt(own_total) + 1e-06))
    return (update, new_mom_rot, new_var_rot, new_mom_plain, new_var_plain)


def solution(mesh):
    return jax.shard_map(
        per_device,
        mesh=mesh,
        in_specs=(
            P("rows", "cols"),
            P("rows", "cols"),
            P("cols", "rows"),
            P("cols", "rows"),
            P("rows", "cols"),
            P("rows", "cols"),
        ),
        out_specs=(
            P("rows", "cols"),
            P("cols", "rows"),
            P("cols", "rows"),
            P("rows", "cols"),
            P("rows", "cols"),
        ),
        check_vma=False,
    )
```

profile of v0, /device:TPU:0, one launch (start us, length us, event | category | flops | bytes accessed | tf_op | source)
XLA Modules:
  0.0 454.9 jit_solution(14724510725478670371)
XLA Ops:
  7.2 0.0 copy-start
  7.2 0.0 all-gather.3.cloned.1.call-start
  7.2 0.7 all-gather.3.cloned.1.call-update
  7.9 0.0 reduce-scatter.3.cloned.1.call-start
  8.0 115.2 %all-gather.3.cloned.1.call-done = f32[896,4096]{1,0:T(8,128)} async-done(((f32[896,256]{1,0:T(8,128)}), f32[896,4096]{1,0:T(8,128)}) %all-gather.3.cloned.1.call-update) | async-done | bytes 14680080 | tf_op jit(solution)/shard_map/all_gather | solution.py:29
  123.1 0.0 copy-done
  123.1 27.4 %fusion.4 = f32[448,4096]{1,0:T(8,128)} fusion(f32[896,448]{0,1:T(8,128)S(1)} %copy-done, f32[896,4096]{1,0:T(8,128)} %all-gather.3.cloned.1.call-done), kind=kOutput, calls=%fused_computation.11 | convolution fusion | flops 19730006016 | bytes 23625728 | tf_op jit(solution)/shard_map/dot_general | solution.py:27
  150.6 0.0 reduce-scatter.3.cloned.1.call-update
  150.6 0.0 all-gather.5.cloned.1.call-start
  150.6 46.7 %reduce-scatter.3.cloned.1.call-done = f32[448,512]{1,0:T(8,128)} async-done(((f32[448,4096]{1,0:T(8,128)}), f32[448,512]{1,0:T(8,128)}) %reduce-scatter.3.cloned.1.call-update) | async-done | bytes 917520 | tf_op jit(solution)/shard_map/reduce_scatter | solution.py:34
  197.4 3.1 add_divide_fusion
  200.5 0.0 all-gather.5.cloned.1.call-update
  200.5 0.2 reduce-scatter.5.cloned.1.call-start
  200.7 44.8 %all-gather.5.cloned.1.call-done = f32[448,4096]{1,0:T(8,128)} async-done(((f32[448,512]{1,0:T(8,128)}), f32[448,4096]{1,0:T(8,128)}) %all-gather.5.cloned.1.call-update) | async-done | bytes 7340048 | tf_op jit(solution)/shard_map/all_gather | solution.py:38
  245.5 30.5 %convolution_bitcast_fusion = f32[896,4096]{0,1:T(8,128)} fusion(f32[448,4096]{1,0:T(8,128)} %all-gather.5.cloned.1.call-done, f32[896,448]{0,1:T(8,128)S(1)} %copy-done), kind=kOutput, calls=%fused_computation | convolution fusion | flops 19730006016 | bytes 23625728 | tf_op jit(solution)/shard_map/dot_general | solution.py:36
  276.1 0.0 reduce-scatter.5.cloned.1.call-update
  276.1 1.2 copy-done.1
  277.2 0.3 copy-done.2
  277.5 3.6 multiply_reduce_fusion.1
  281.1 97.2 %reduce-scatter.5.cloned.1.call-done = f32[896,256]{0,1:T(8,128)} async-done(((f32[896,4096]{0,1:T(8,128)}), f32[896,256]{0,1:T(8,128)}) %reduce-scatter.5.cloned.1.call-update) | async-done | bytes 917520 | tf_op jit(solution)/shard_map/reduce_scatter | solution.py:42
  378.3 2.0 multiply_reduce_fusion
  380.3 64.3 %all-reduce = (f32[]{:T(128)}, f32[]{:T(128)}) all-reduce(f32[]{:T(128)} %get-tuple-element.12, f32[]{:T(128)} %multiply_reduce_fusion), channel_id=1, replica_groups=mesh['rows'=8,'cols'=16] {'rows','cols'}, use_global_device_ids=true, to_apply=%region_3.0 | all-reduce | flops 2 | bytes 16 | tf_op jit(solution)/shard_map/psum | solution.py:26
  445.9 1.2 broadcast_multiply_fusion
  447.1 1.2 copy.11
  (6 shorter events, 0.0 us)
Async XLA Ops:
  7.2 116.0 %copy-start = (f32[896,448]{0,1:T(8,128)S(1)}, f32[896,448]{0,1:T(8,128)}, u32[]{:S(2)}) copy-start(f32[896,448]{0,1:T(8,128)} %param.7) | copy-start | bytes 4816900
  7.2 116.0 %all-gather.3.cloned.1.call-start = ((), (), s32[]{:S(2)}) async-start(), calls=%async_computation.2 | async-start | bytes 15597568 | tf_op jit(solution)/shard_map/all_gather | solution.py:29
  7.9 189.5 %reduce-scatter.3.cloned.1.call-start = ((), (), s32[]{:S(2)}) async-start(), calls=%async_computation.3 | async-start | bytes 8257536 | tf_op jit(solution)/shard_map/reduce_scatter | solution.py:34
  150.6 46.8 %copy-start.3 = (f32[448,512]{1,0:T(8,128)S(1)}, f32[448,512]{1,0:T(8,128)}, u32[]{:S(2)}) copy-start(f32[448,512]{1,0:T(8,128)} %param.8) | copy-start | bytes 2752516
  150.6 46.8 %copy-start.4 = (f32[448,512]{1,0:T(8,128)S(1)}, f32[448,512]{1,0:T(8,128)}, u32[]{:S(2)}) copy-start(f32[448,512]{1,0:T(8,128)} %param.9) | copy-start | bytes 2752516
  150.6 94.9 %all-gather.5.cloned.1.call-start = ((), (), s32[]{:S(2)}) async-start(), calls=%async_computation.4 | async-start | bytes 8257536 | tf_op jit(solution)/shard_map/all_gather | solution.py:38
  200.5 177.7 %reduce-scatter.5.cloned.1.call-start = ((), (), s32[]{:S(2)}) async-start(), calls=%async_computation.5 | async-start | bytes 15597568 | tf_op jit(solution)/shard_map/reduce_scatter | solution.py:42
  276.1 1.2 copy-start.1
  276.1 1.5 copy-start.2
Sparse Core Ops, SparseCore 0:
  10.1 112.9 all-gather.2
  150.7 46.6 reduce-scatter.2
  200.6 44.8 all-gather.4
  276.2 101.9 reduce-scatter.4
where the time goes:
time: 456 us; the launch traced here: 455 us
  waiting for transfers between devices  305 us (67%)
  blocking collectives  64.3 us (14%)
  matrix products  57.9 us (13%)
  between operations  15.1 us (3%)
  other arithmetic  9.92 us (2%)
    all_gather x1, waiting for transfers between devices, per_device(): lax.all_gather(grad, 'cols', axis=1, tiled=True)  115 us
    reduce_scatter x1, waiting for transfers between devices, per_device(): lax.psum_scatter(partial_back, 'cols', scatter_dimension=1, tiled=True)  97.2 us
    psum x1, blocking collectives, per_device(): graft_total = lax.psum(plain_local, ('rows', 'cols'))  64.3 us
    reduce_scatter x1, waiting for transfers between devices, per_device(): lax.psum_scatter(partial_rot, 'rows', scatter_dimension=1, tiled=True)  46.7 us
    all_gather x1, waiting for transfers between devices, per_device(): lax.all_gather(direction, 'rows', axis=1, tiled=True)  44.8 us
    dot_general x1, matrix products, per_device(): jnp.dot(basis, lax.all_gather(direction, 'rows', axis=1, tiled=True), pre...  30.5 us
    dot_general x1, matrix products, per_device(): lax.dot_general(basis, lax.all_gather(grad, 'cols', axis=1, tiled=True),...  27.4 us
  transfers between devices with their start and end apart: 4, of which 4 were waited for; matrix products, arithmetic and copies ran while one was open for 1% of the time, Pallas kernels for 0%

commit v1 on v0

v1 whole, which is shorter than its diff:
```python
import functools

import jax
import jax.numpy as jnp
from jax import lax
from jax.experimental import pallas as pl
from jax.experimental.pallas import tpu as pltpu
from jax.sharding import PartitionSpec as P

STEP = 10
BETA = 0.95
EPS = 1e-08
CORR = 1.0 - BETA**STEP

F32 = jnp.float32
BF16 = jnp.bfloat16

KI = 896
KJ = 448
KN = 256
HJ = KJ // 2
HALF = HJ // 2
OFF = (0, 1, 3, 2)
N_COPIES = 96


def adam(moment, second, values):
    moment_new = BETA * moment + (1.0 - BETA) * values
    second_new = BETA * second + (1.0 - BETA) * values * values
    direction = moment_new / CORR / (jnp.sqrt(second_new / CORR) + EPS)
    return moment_new, second_new, direction


def split(a):
    hi = a.astype(BF16)
    lo = (a - hi.astype(F32)).astype(BF16)
    return hi, lo


def dot3(lh, ll, rh, rl):
    dot = functools.partial(jnp.dot, preferred_element_type=F32)
    return dot(lh, rh) + (dot(lh, rl) + dot(ll, rh))


def kernel(
    grad, basis, mom_rot, var_rot, mom_plain, var_plain,
    update, new_mom_rot, new_var_rot, new_mom_plain, new_var_plain,
    gg, ghi, glo, bg, bhi, blo, bthi, btlo, part, rx, ra, rb, rt, at,
    m2, v2, direc, dd, dhi, dlo, back, ya, yb, mp, vp, norm, nrecv,
    ssem, rsem, lsem,
):
    rows = lax.axis_index("rows")
    cols = lax.axis_index("cols")
    x, c = rows // 2, rows % 2
    y, z = cols // 4, cols % 4
    o = 1 - c

    def dev(dx=0, dc=0, dy=0, dz=0):
        r = (x + dx) % 4 * 2 + (c + dc) % 2
        q = (y + dy) % 4 * 4 + (z + dz) % 4
        return (r, q)

    xp, xm, xo = (x + 1) % 4, (x + 3) % 4, (x + 2) % 4
    yp, ym, yo = (y + 1) % 4, (y + 3) % 4, (y + 2) % 4
    mine = pl.multiple_of(c * HJ, HJ)
    other = pl.multiple_of(o * HJ, HJ)

    partners = [dev(dc=1)]
    for d in (1, 2, 3):
        partners += [dev(dx=d), dev(dy=d), dev(dz=d)]
    barrier = pltpu.get_barrier_semaphore()
    for p in partners:
        pl.semaphore_signal(barrier, inc=1, device_id=p, device_id_type=pl.DeviceIdType.MESH)
    pl.semaphore_wait(barrier, len(partners))

    count = [0, 0]
    started = []

    def send(src, dst, to):
        i = count[0]
        count[0] += 1
        copy = pltpu.make_async_remote_copy(
            src_ref=src, dst_ref=dst, send_sem=ssem.at[i], recv_sem=rsem.at[i],
            device_id=to, device_id_type=pl.DeviceIdType.MESH,
        )
        copy.start()
        started.append(copy)
        return copy

    def local(src, dst):
        i = count[1]
        count[1] += 1
        copy = pltpu.make_async_copy(src, dst, lsem.at[i])
        copy.start()
        return copy

    g_up = send(grad, gg.at[y], dev(dy=1))
    g_dn = send(grad, gg.at[y], dev(dy=3))
    b_up = send(basis, bg.at[2], dev(dz=1))
    b_dn = send(basis, bg.at[1], dev(dz=3))
    own_g = local(grad, gg.at[y])
    own_b = local(basis, bg.at[0])
    own_plain = [local(mom_plain, mp), local(var_plain, vp)]
    moments = []
    for t in range(2):
        for src, dst in ((mom_rot, m2), (var_rot, v2)):
            lanes = pl.ds(t * KN, KN)
            moments.append(send(src.at[pl.ds(other, HJ), lanes], dst.at[2 * c + t], dev(dc=1)))
    moments_own = []
    for t in range(2):
        for src, dst in ((mom_rot, m2), (var_rot, v2)):
            lanes = pl.ds(t * KN, KN)
            moments_own.append(local(src.at[pl.ds(mine, HJ), lanes], dst.at[2 * c + t]))

    own_g.wait()
    for copy in own_plain:
        copy.wait()
    norm[...] = jnp.zeros_like(norm)

    @pl.loop(0, KI // 64)
    def _(i):
        s = pl.ds(pl.multiple_of(i * 64, 64), 64)
        m, v, d = adam(mp[s, :], vp[s, :], gg[y, s, :])
        mp[s, :] = m
        vp[s, :] = v
        norm[0] += jnp.sum((d * d).reshape(8, 8, KN), axis=0)

    out_plain = [local(mp, new_mom_plain), local(vp, new_var_plain)]

    def split_grad(n):
        @pl.loop(0, KI // 128)
        def _(i):
            s = pl.ds(pl.multiple_of(i * 128, 128), 128)
            hi, lo = split(gg[n, s, :])
            ghi[n, s, :] = hi
            glo[n, s, :] = lo

    def turn_basis(r):
        for q in range(0, KJ, 128):
            w = min(128, KJ - q)
            hi, lo = split(bg[r, :, q:q + w].T)
            bthi[q:q + w, :] = hi
            btlo[q:q + w, :] = lo

    def product_one(r):
        @pl.loop(0, 4)
        def _(n):
            part[r, n] = dot3(bthi[...], btlo[...], ghi[n], glo[n])

    split_grad(y)
    own_b.wait()
    turn_basis(0)
    g_up.wait_recv()
    g_dn.wait_recv()
    g_up2 = send(gg.at[ym, pl.ds(0, KI // 2)], gg.at[ym, pl.ds(0, KI // 2)], dev(dy=1))
    g_dn2 = send(gg.at[yp, pl.ds(KI // 2, KI // 2)], gg.at[yp, pl.ds(KI // 2, KI // 2)], dev(dy=3))
    split_grad(ym)
    split_grad(yp)
    g_up2.wait_recv()
    g_dn2.wait_recv()
    split_grad(yo)

    state = {}

    def s0(r):
        if r == 1:
            b_up.wait_recv()
            b_dn.wait_recv()
            top, low = pl.ds(0, KI // 2), pl.ds(KI // 2, KI // 2)
            state["b2"] = (
                send(bg.at[2, top], bg.at[3, top], dev(dz=1)),
                send(bg.at[1, low], bg.at[3, low], dev(dz=3)),
            )
        if r == 3:
            for copy in state["b2"]:
                copy.wait_recv()
        if r:
            turn_basis(r)
        product_one(r)
        state["x", r] = send(part.at[r, :, pl.ds(other, HJ)], rx.at[r], dev(dc=1))

    def s1(r):
        state["x", r].wait_recv()

        @pl.loop(0, 4)
        def _(n):
            part[r, n, pl.ds(mine, HJ), :] += rx[r, n]

        first = part.at[r, xo, pl.ds(mine, HALF)]
        second = part.at[r, xo, pl.ds(mine + HALF, HALF)]
        state["ra", r] = (send(first, ra.at[r, 0], dev(dx=1)), send(second, ra.at[r, 1], dev(dx=3)))

    def s2(r):
        up, dn = state["ra", r]
        up.wait_recv()
        part[r, xp, pl.ds(mine, HALF), :] += ra[r, 0]
        a = send(part.at[r, xp, pl.ds(mine, HJ)], rb.at[r, 0], dev(dx=1))
        dn.wait_recv()
        part[r, xm, pl.ds(mine + HALF, HALF), :] += ra[r, 1]
        b = send(part.at[r, xm, pl.ds(mine, HJ)], rb.at[r, 1], dev(dx=3))
        state["rb", r] = (a, b)

    def s3(r):
        for copy in state["rb", r]:
            copy.wait_recv()
        rt[r] = part[r, x, pl.ds(mine, HJ), :] + rb[r, 0] + rb[r, 1]
        if r:
            state["at", r] = send(rt.at[r], at.at[r], dev(dz=OFF[r]))

    def s4(r):
        if r == 0:
            for copy in moments:
                copy.wait_recv()
            for copy in moments_own:
                copy.wait()
            values = rt[r]
        else:
            state["at", r].wait_recv()
            values = at[r]
        zs = (z + 4 - OFF[r]) % 4
        m, v, d = adam(m2[zs], v2[zs], values)
        m2[zs] = m
        v2[zs] = v
        if r == 0:
            dd[r, x, pl.ds(mine, HJ), :] = d
        else:
            direc[r] = d
            state["d", r] = send(direc.at[r], dd.at[r, x, pl.ds(mine, HJ)], dev(dz=4 - OFF[r]))

    def tile(r, n):
        return dd.at[r, n, pl.ds(mine, HJ)]

    def s5(r):
        if r:
            state["d", r].wait_recv()
        state["ag", r] = (
            send(tile(r, x), tile(r, x), dev(dx=1)),
            send(tile(r, x), tile(r, x), dev(dx=3)),
        )
        state["dc", r] = [send(tile(r, x), tile(r, x), dev(dc=1))]

    def s6(r):
        up, dn = state["ag", r]
        up.wait_recv()
        first = dd.at[r, xm, pl.ds(mine, HALF)]
        a = send(first, first, dev(dx=1))
        dn.wait_recv()
        second = dd.at[r, xp, pl.ds(mine + HALF, HALF)]
        b = send(second, second, dev(dx=3))
        state["ag2", r] = (a, b)
        state["dc", r].append(send(tile(r, xm), tile(r, xm), dev(dc=1)))
        state["dc", r].append(send(tile(r, xp), tile(r, xp), dev(dc=1)))

    def s7(r):
        for copy in state["ag2", r]:
            copy.wait_recv()
        state["dc", r].append(send(tile(r, xo), tile(r, xo), dev(dc=1)))

    def s8(r, first, last):
        for copy in state["dc", r]:
            copy.wait_recv()

        @pl.loop(0, KI // 64)
        def _(i):
            s = pl.ds(pl.multiple_of(i * 64, 64), 64)
            hi, lo = split(bg[r, s, :])
            bhi[s, :] = hi
            blo[s, :] = lo

        @pl.loop(0, 4)
        def _(n):
            hi, lo = split(dd[r, n])
            dhi[n] = hi
            dlo[n] = lo

        def one(n):
            new = dot3(bhi[...], blo[...], dhi[n], dlo[n])
            back[n] = new if first else back[n] + new

        if not last:
            pl.loop(0, 4)(one)
            return
        top, low = pl.ds(0, KI // 2), pl.ds(KI // 2, KI // 2)
        one(yo)
        up = send(back.at[yo, top], ya.at[0], dev(dy=1))
        dn = send(back.at[yo, low], ya.at[1], dev(dy=3))
        one(yp)
        one(ym)
        up.wait_recv()
        back[yp, top, :] += ya[0]
        up2 = send(back.at[yp], yb.at[0], dev(dy=1))
        dn.wait_recv()
        back[ym, low, :] += ya[1]
        dn2 = send(back.at[ym], yb.at[1], dev(dy=3))
        one(y)
        state["yb"] = (up2, dn2)

    order = [
        (s0, 0), (s0, 1), (s1, 0), (s0, 2), (s2, 0), (s1, 1), (s3, 0), (s4, 0), (s5, 0),
        (s2, 1), (s1, 2), (s3, 1), (s2, 2), (s4, 1), (s3, 2), (s6, 0), (s4, 2), (s5, 1), (s5, 2),
        (s0, 3), (s7, 0), (s6, 1), (s1, 3), (s7, 1), (s6, 2), (s2, 3), (s7, 2),
        (s3, 3), (s8, 0), (s4, 3), (s8, 1), (s5, 3), (s8, 2), (s6, 3), (s7, 3), (s8, 3),
    ]
    for stage, r in order:
        if stage is s8:
            s8(r, first=r == 0, last=r == 3)
        else:
            stage(r)

    lanes = [pl.ds(t * KN, KN) for t in range(2)]
    out_rot, out_rot_own = [], []
    for t in range(2):
        for src, dst in ((m2, new_mom_rot), (v2, new_var_rot)):
            out_rot.append(send(src.at[2 * o + t], dst.at[pl.ds(mine, HJ), lanes[t]], dev(dc=1)))
            out_rot_own.append(local(src.at[2 * c + t], dst.at[pl.ds(mine, HJ), lanes[t]]))

    for copy in state["yb"]:
        copy.wait_recv()

    @pl.loop(0, KI // 64)
    def _(i):
        s = pl.ds(pl.multiple_of(i * 64, 64), 64)
        b = back[y, s, :] + yb[0, s, :] + yb[1, s, :]
        back[y, s, :] = b
        norm[1] += jnp.sum((b * b).reshape(8, 8, KN), axis=0)

    slot = 0
    for moves in (
        [dev(dc=1)],
        [dev(dx=d) for d in (1, 2, 3)],
        [dev(dy=d) for d in (1, 2, 3)],
        [dev(dz=d) for d in (1, 2, 3)],
    ):
        copies = []
        for to in moves:
            copies.append((slot, send(norm, nrecv.at[slot], to)))
            slot += 1
        for _, copy in copies:
            copy.wait()
        started[:] = [s for s in started if all(s is not copy for _, copy in copies)]
        total = norm[...]
        for k, _ in copies:
            total += nrecv[k]
        norm[...] = total
    graft = jnp.sqrt(jnp.sum(norm[0], keepdims=True))
    own = jnp.sqrt(jnp.sum(norm[1], keepdims=True))
    scale = graft / (own + 1e-06)

    for copy in out_plain:
        copy.wait()

    @pl.loop(0, KI // 64)
    def _(i):
        s = pl.ds(pl.multiple_of(i * 64, 64), 64)
        mp[s, :] = back[y, s, :] * scale

    last = local(mp, update)
    for copy in started:
        copy.wait_send()
    for copy in out_rot:
        copy.wait_recv()
    for copy in out_rot_own:
        copy.wait()
    last.wait()


def per_device(grad, basis, mom_rot, var_rot, mom_plain, var_plain):
    plain = jax.ShapeDtypeStruct((KI, KN), F32)
    rot = jax.ShapeDtypeStruct((KJ, 2 * KN), F32)
    scratch = [
        pltpu.VMEM((4, KI, KN), F32),
        pltpu.VMEM((4, KI, KN), BF16),
        pltpu.VMEM((4, KI, KN), BF16),
        pltpu.VMEM((4, KI, KJ), F32),
        pltpu.VMEM((KI, KJ), BF16),
        pltpu.VMEM((KI, KJ), BF16),
        pltpu.VMEM((KJ, KI), BF16),
        pltpu.VMEM((KJ, KI), BF16),
        pltpu.VMEM((4, 4, KJ, KN), F32),
        pltpu.VMEM((4, 4, HJ, KN), F32),
        pltpu.VMEM((4, 2, HALF, KN), F32),
        pltpu.VMEM((4, 2, HJ, KN), F32),
        pltpu.VMEM((4, HJ, KN), F32),
        pltpu.VMEM((4, HJ, KN), F32),
        pltpu.VMEM((4, HJ, KN), F32),
        pltpu.VMEM((4, HJ, KN), F32),
        pltpu.VMEM((4, HJ, KN), F32),
        pltpu.VMEM((4, 4, KJ, KN), F32),
        pltpu.VMEM((4, KJ, KN), BF16),
        pltpu.VMEM((4, KJ, KN), BF16),
        pltpu.VMEM((4, KI, KN), F32),
        pltpu.VMEM((2, KI // 2, KN), F32),
        pltpu.VMEM((2, KI, KN), F32),
        pltpu.VMEM((KI, KN), F32),
        pltpu.VMEM((KI, KN), F32),
        pltpu.VMEM((2, 8, KN), F32),
        pltpu.VMEM((10, 2, 8, KN), F32),
        pltpu.SemaphoreType.DMA((N_COPIES,)),
        pltpu.SemaphoreType.DMA((N_COPIES,)),
        pltpu.SemaphoreType.DMA((24,)),
    ]
    return pl.pallas_call(
        kernel,
        out_shape=(plain, rot, rot, plain, plain),
        in_specs=[pl.BlockSpec(memory_space=pl.ANY)] * 6,
        out_specs=[pl.BlockSpec(memory_space=pl.ANY)] * 5,
        scratch_shapes=scratch,
        compiler_params=pltpu.CompilerParams(
            collective_id=0, has_side_effects=True, vmem_limit_bytes=63 * 1024 * 1024
        ),
        cost_estimate=pl.CostEstimate(flops=20_000_000_000, bytes_accessed=12_000_000, transcendentals=0),
    )(grad, basis, mom_rot, var_rot, mom_plain, var_plain)


def solution(mesh):
    return jax.shard_map(
        per_device,
        mesh=mesh,
        in_specs=(
            P("rows", "cols"),
            P("rows", "cols"),
            P("cols", "rows"),
            P("cols", "rows"),
            P("rows", "cols"),
            P("rows", "cols"),
        ),
        out_specs=(
            P("rows", "cols"),
            P("cols", "rows"),
            P("cols", "rows"),
            P("rows", "cols"),
            P("rows", "cols"),
        ),
        check_vma=False,
    )
```

time: 456 us -> 201 us (0.44)
  waiting for transfers between devices: 305 us -> 0 us
  Pallas kernels: 0 us -> 191 us
  blocking collectives: 64.3 us -> 0 us
  matrix products: 57.9 us -> 0 us
  between operations: 15.1 us -> 0.66 us
  other arithmetic: 9.92 us -> 0 us
  local copies, waits for them, and re-layouts: 2.67 us -> 8.81 us
    pallas_call x0 -> x1, Pallas kernels: none -> 191 us  [per_device(): pl.pallas_call(kernel, out_shape=(plain, rot, rot, plain, plain), in_spec...]
    all_gather x2 -> x0, waiting for transfers between devices: 160 us -> none  [the longest x1 115 us: per_device(): lax.all_gather(grad, 'cols', axis=1, tiled=True)]
    reduce_scatter x2 -> x0, waiting for transfers between devices: 144 us -> none  [the longest x1 97.2 us: per_device(): lax.psum_scatter(partial_back, 'cols', scatter_dimension=1, tiled=True)]
    psum x1 -> x0, blocking collectives: 64.3 us -> none  [per_device(): graft_total = lax.psum(plain_local, ('rows', 'cols'))]
    dot_general x2 -> x0, matrix products: 57.9 us -> none  [the longest x1 30.5 us: per_device(): jnp.dot(basis, lax.all_gather(direction, 'rows', axis=1, tiled=True), pre...]
    unnamed x11 -> x14, local copies, waits for them, and re-layouts: 2.67 us -> 8.81 us
    reduce_sum x2 -> x0, other arithmetic: 5.6 us -> none  [the longest x1 3.59 us: per_device(): plain_local = jnp.sum(plain * plain)]
  transfers between devices with their start and end apart: 4 -> 0, of which waited for: 4 -> 0; matrix products, arithmetic and copies ran while one was open for 1% -> 0% of each run, Pallas kernels for 0% -> 0%
where the time goes in v1:
time: 201 us; the launch traced here: 200 us
  Pallas kernels  191 us (95%)
  local copies, waits for them, and re-layouts  8.81 us (4%)
    pallas_call x1, Pallas kernels, per_device(): pl.pallas_call(kernel, out_shape=(plain, rot, rot, plain, plain), in_spec...  191 us
    unnamed x14, local copies, waits for them, and re-layouts  8.81 us

profile of v1, /device:TPU:0, one launch (start us, length us, event | category | flops | bytes accessed | tf_op | source)
XLA Modules:
  0.0 200.5 jit_solution(13590946656731065362)
XLA Ops:
  0.6 2.8 %copy.11.basis = f32[896,448]{1,0:T(8,128)} copy(f32[896,448]{0,1:T(8,128)} %param.7) | data formatting | bytes 3211264 | tf_op args[1]
  3.4 191.0 %shard_map.101 = (f32[896,256]{1,0:T(8,128)}, f32[448,512]{1,0:T(8,128)}, f32[448,512]{1,0:T(8,128)}, f32[896,256]{1,0:T(8,128)}, f32[896,256]{1,0:T(8,128)}) custom-call(f32[896,256]{1,0:T(8,128)} %grad.1, f32[896,448]{1,0:T(8,128)} %copy.11.basis, f32[448,512]{1,0:T(8,128)} %mom_rot.1, f32[448,512]{1,0:T(8,128)} %var_rot.1, f32[896,256]{1,0:T(8,128)} %mom_plain.1, ...), custom_call_target="tpu_custom_call" | custom-call | flops 20000000000 | bytes 12000000 | tf_op jit(solution)/shard_map/pallas_call | solution.py:402
  194.5 0.0 copy-start.3
  194.5 0.0 copy-start.2
  194.5 2.3 %copy.17 = f32[896,256]{1,0:T(8,128)} copy(f32[896,256]{1,0:T(8,128)} %get-tuple-element.10) | data formatting | bytes 1835008
  196.8 0.0 copy-done.3
  196.8 0.0 copy-start.1
  196.8 0.9 copy.18
  197.7 0.0 copy-done.2
  197.7 0.0 copy-start
  197.7 0.9 copy.19
  198.6 0.0 copy-done.1
  198.6 0.9 copy.20
  199.6 0.0 copy-done
  199.6 0.9 copy.21
Async XLA Ops:
  194.5 2.3 %copy-start.3 = (f32[448,512]{1,0:T(8,128)S(1)}, f32[448,512]{1,0:T(8,128)}, u32[]{:S(2)}) copy-start(f32[448,512]{1,0:T(8,128)} %get-tuple-element.11) | copy-start | bytes 2752516
  194.5 3.2 %copy-start.2 = (f32[448,512]{1,0:T(8,128)S(1)}, f32[448,512]{1,0:T(8,128)}, u32[]{:S(2)}) copy-start(f32[448,512]{1,0:T(8,128)} %get-tuple-element.12) | copy-start | bytes 2752516
  196.8 1.9 copy-start.1
  197.7 1.9 copy-start

commit v2 on v0

v2 whole, which is shorter than its diff:
```python
import functools

import jax
import jax.numpy as jnp
from jax import lax
from jax.experimental import pallas as pl
from jax.experimental.pallas import tpu as pltpu
from jax.sharding import PartitionSpec as P

STEP = 10
BETA = 0.95
EPS = 1e-08
CORR = 1.0 - BETA**STEP

F32 = jnp.float32
BF16 = jnp.bfloat16

KI = 896
KJ = 448
KN = 256
QJ = KJ // 2
HN = KN // 2
CJ = QJ // 2
CHUNKS = ((0, 0), (0, 1), (1, 1), (3, 0), (1, 0), (3, 1), (2, 0), (2, 1))
GROUPS = ((0, 2), (2, 4), (4, 6), (6, 7), (7, 8))
N_COPIES = 176


def adam(moment, second, values):
    moment_new = BETA * moment + (1.0 - BETA) * values
    second_new = BETA * second + (1.0 - BETA) * values * values
    direction = moment_new / CORR / (jnp.sqrt(second_new / CORR) + EPS)
    return moment_new, second_new, direction


def split(a):
    hi = a.astype(BF16)
    lo = (a - hi.astype(F32)).astype(BF16)
    return hi, lo


def dot3(lh, ll, rh, rl):
    dot = functools.partial(jnp.dot, preferred_element_type=F32)
    return dot(lh, rh) + (dot(lh, rl) + dot(ll, rh))


def kernel(
    grad, basis_t, mom_rot, var_rot, mom_plain, var_plain,
    out_back, out_norm, new_mom_rot, new_var_rot, new_mom_plain, new_var_plain,
    gg, ghi, glo, bt, lhi, llo, bhi, blo, part, rx, ra, rb, rt, at,
    m2, v2, direc, dd, dhi, dlo, back, ya, yb, mp, vp, norm, nrecv,
    ssem, rsem, lsem,
):
    rows = lax.axis_index("rows")
    cols = lax.axis_index("cols")
    x, c = rows // 2, rows % 2
    y, z = cols // 4, cols % 4
    o = 1 - c

    def dev(dx=0, dc=0, dy=0, dz=0):
        r = (x + dx) % 4 * 2 + (c + dc) % 2
        q = (y + dy) % 4 * 4 + (z + dz) % 4
        return (r, q)

    xp, xm, xo = (x + 1) % 4, (x + 3) % 4, (x + 2) % 4
    yp, ym, yo = (y + 1) % 4, (y + 3) % 4, (y + 2) % 4
    mine = pl.ds(pl.multiple_of(c * CJ, CJ), CJ)
    other = pl.ds(pl.multiple_of(o * CJ, CJ), CJ)
    top, low = pl.ds(0, KI // 2), pl.ds(KI // 2, KI // 2)

    norm_moves = (
        [dev(dc=1)] + [dev(dx=d, dc=e) for d in (1, 2, 3) for e in (0, 1)],
        [dev(dy=d) for d in (1, 2, 3)],
        [dev(dz=d) for d in (1, 2, 3)],
    )
    partners = [p for moves in norm_moves for p in moves]
    barrier = pltpu.get_barrier_semaphore()
    for p in partners:
        pl.semaphore_signal(barrier, inc=1, device_id=p, device_id_type=pl.DeviceIdType.MESH)
    pl.semaphore_wait(barrier, len(partners))

    count = [0, 0]
    started = []

    def send(src, dst, to):
        i = count[0]
        count[0] += 1
        copy = pltpu.make_async_remote_copy(
            src_ref=src, dst_ref=dst, send_sem=ssem.at[i], recv_sem=rsem.at[i],
            device_id=to, device_id_type=pl.DeviceIdType.MESH,
        )
        copy.start()
        started.append(copy)
        return copy

    def local(src, dst):
        i = count[1]
        count[1] += 1
        copy = pltpu.make_async_copy(src, dst, lsem.at[i])
        copy.start()
        return copy

    state = {}

    def arrived(key):
        for copy in state.pop(key, ()):
            copy.wait_recv()

    def chunk(i):
        return bt.at[pl.ds(i * QJ, QJ)]

    def gather_grad(h):
        own = grad.at[:, pl.ds(h * HN, HN)]
        state["g", h] = [send(own, gg.at[h, y], dev(dy=1)), send(own, gg.at[h, y], dev(dy=3))]

    gather_grad(0)
    halves = [basis_t.at[pl.ds(q * QJ, QJ)] for q in range(2)]
    state["b", 3] = [send(halves[0], chunk(3), dev(dz=1))]
    state["b", 2] = [send(halves[1], chunk(2), dev(dz=3))]
    state["b", 5] = [send(halves[1], chunk(5), dev(dz=1))]
    state["b", 4] = [send(halves[0], chunk(4), dev(dz=3))]
    own_g = [local(grad.at[:, pl.ds(h * HN, HN)], gg.at[h, y]) for h in range(2)]
    own_b = [local(basis_t, bt.at[pl.ds(0, KJ)])]
    own_plain = [local(mom_plain, mp), local(var_plain, vp)]
    state["mv"] = [send(src.at[:, other], dst.at[c], dev(dc=1)) for src, dst in ((mom_rot, m2), (var_rot, v2))]
    own_mv = [local(src.at[:, mine], dst.at[c]) for src, dst in ((mom_rot, m2), (var_rot, v2))]

    norm[...] = jnp.zeros_like(norm)
    out_plain = []

    def done(copies):
        while copies:
            copies.pop().wait()

    def plain():
        done(own_g)
        done(own_plain)

        @pl.loop(0, KI // 64)
        def _(i):
            s = pl.ds(pl.multiple_of(i * 64, 64), 64)
            for h in range(2):
                lanes = slice(h * HN, (h + 1) * HN)
                m, v, d = adam(mp[s, lanes], vp[s, lanes], gg[h, y, s, :])
                mp[s, lanes] = m
                vp[s, lanes] = v
                norm[0] += jnp.sum((d * d).reshape(8, 8, HN), axis=0)

        out_plain.append(local(mp, new_mom_plain))
        out_plain.append(local(vp, new_var_plain))

    def split_grad(h, n):
        @pl.loop(0, KI // 128)
        def _(i):
            s = pl.ds(pl.multiple_of(i * 128, 128), 128)
            hi, lo = split(gg[h, n, s, :])
            ghi[h, n, s, :] = hi
            glo[h, n, s, :] = lo

    def gf(h):
        up, dn = state.pop(("g", h))
        up.wait_recv()
        a = send(gg.at[h, ym, top], gg.at[h, ym, top], dev(dy=1))
        dn.wait_recv()
        b = send(gg.at[h, yp, low], gg.at[h, yp, low], dev(dy=3))
        state["g2", h] = [a, b]
        if h == 0:
            gather_grad(1)

    def gs(h):
        done(own_g)
        for n in (y, ym, yp):
            split_grad(h, n)

    def gs2(h):
        arrived(("g2", h))
        split_grad(h, yo)

    def bf(way):
        if way == 0:
            arrived(("b", 3))
            state["b", 6] = [send(chunk(3), chunk(6), dev(dz=1))]
        else:
            arrived(("b", 2))
            state["b", 7] = [send(chunk(2), chunk(7), dev(dz=3))]

    def basis_there(lo, hi):
        for i in range(lo, hi):
            if i < 2:
                done(own_b)
            arrived(("b", i))

    def away(g):
        return [i for i in range(*GROUPS[g]) if CHUNKS[i][0]]

    def ways(g):
        lo, hi = GROUPS[g]
        if hi - lo == 2:
            return [(pl.ds(lo, 1), mine), (pl.ds(lo + 1, 1), mine)]
        start = pl.multiple_of(c * CJ, CJ)
        return [
            (pl.ds(lo, 1), pl.ds(start, CJ // 2)),
            (pl.ds(lo, 1), pl.ds(pl.multiple_of(start + CJ // 2, CJ // 2), CJ // 2)),
        ]

    def ways_share(g):
        lo, hi = GROUPS[g]
        if hi - lo == 2:
            return [(pl.ds(lo, 1), pl.ds(0, CJ)), (pl.ds(lo + 1, 1), pl.ds(0, CJ))]
        return [(pl.ds(lo, 1), pl.ds(0, CJ // 2)), (pl.ds(lo, 1), pl.ds(CJ // 2, CJ // 2))]

    def s0(g, h):
        lo, hi = GROUPS[g]
        basis_there(lo, hi)
        size = (hi - lo) * QJ
        high, rest = split(bt[lo * QJ:hi * QJ, :])
        lhi[:size, :] = high
        llo[:size, :] = rest

        @pl.loop(0, 2)
        def _(p):
            rh = jnp.concatenate([ghi[h, 2 * p], ghi[h, 2 * p + 1]], axis=1)
            rl = jnp.concatenate([glo[h, 2 * p], glo[h, 2 * p + 1]], axis=1)
            new = dot3(lhi[:size, :], llo[:size, :], rh, rl)
            for i in range(hi - lo):
                part[h, 2 * p, lo + i] = new[i * QJ:(i + 1) * QJ, :HN]
                part[h, 2 * p + 1, lo + i] = new[i * QJ:(i + 1) * QJ, HN:]

        group = pl.ds(lo, hi - lo)
        state["x", g, h] = [send(part.at[h, :, group, other], rx.at[h, :, group], dev(dc=1))]

    def s1(g, h):
        lo, hi = GROUPS[g]
        arrived(("x", g, h))
        group = pl.ds(lo, hi - lo)
        for n in range(4):
            part[h, n, group, mine, :] += rx[h, n, group]
        (first, up), (second, dn) = ways(g)
        (first_r, up_r), (second_r, dn_r) = ways_share(g)
        state["ra", g, h] = [
            send(part.at[h, xo, first, up], ra.at[h, 0, first_r, up_r], dev(dx=1)),
            send(part.at[h, xo, second, dn], ra.at[h, 1, second_r, dn_r], dev(dx=3)),
        ]

    def s2(g, h):
        lo, hi = GROUPS[g]
        group = pl.ds(lo, hi - lo)
        (first, up), (second, dn) = ways(g)
        (first_r, up_r), (second_r, dn_r) = ways_share(g)
        a, b = state.pop(("ra", g, h))
        a.wait_recv()
        part[h, xp, first, up, :] += ra[h, 0, first_r, up_r, :]
        a = send(part.at[h, xp, group, mine], rb.at[h, 0, group], dev(dx=1))
        b.wait_recv()
        part[h, xm, second, dn, :] += ra[h, 1, second_r, dn_r, :]
        b = send(part.at[h, xm, group, mine], rb.at[h, 1, group], dev(dx=3))
        state["rb", g, h] = [a, b]

    def s3(g, h):
        lo, hi = GROUPS[g]
        group = pl.ds(lo, hi - lo)
        arrived(("rb", g, h))
        rt[h, group] = part[h, x, group, mine, :] + rb[h, 0, group] + rb[h, 1, group]
        for i in away(g):
            state["at", i, h] = [send(rt.at[h, i], at.at[h, i], dev(dz=CHUNKS[i][0]))]

    def s4(g, h):
        arrived("mv")
        done(own_mv)
        for i in range(*GROUPS[g]):
            off, q = CHUNKS[i]
            arrived(("at", i, h))
            values = at[h, i] if off else rt[h, i]
            zs = (z + 4 - off) % 4
            half = zs // 2
            lanes = pl.ds(pl.multiple_of(zs % 2 * KN + h * HN, HN), HN)
            m, v, d = adam(m2[half, q, :, lanes], v2[half, q, :, lanes], values)
            m2[half, q, :, lanes] = m
            v2[half, q, :, lanes] = v
            if off:
                direc[h, i] = d
                state["d", i, h] = [send(direc.at[h, i], dd.at[h, x, i, mine], dev(dz=4 - off))]
            else:
                dd[h, x, i, mine, :] = d

    def s5(g, h):
        lo, hi = GROUPS[g]
        for i in away(g):
            arrived(("d", i, h))
        t = dd.at[h, x, pl.ds(lo, hi - lo), mine]
        state["ag", g, h] = [send(t, t, dev(dx=1)), send(t, t, dev(dx=3))]

    def s6(g, h):
        (first, up), (second, dn) = ways(g)
        a, b = state.pop(("ag", g, h))
        a.wait_recv()
        t = dd.at[h, xm, first, up]
        a = send(t, t, dev(dx=1))
        b.wait_recv()
        t = dd.at[h, xp, second, dn]
        b = send(t, t, dev(dx=3))
        state["ag2", g, h] = [a, b]

    def s7(g, h):
        lo, hi = GROUPS[g]
        arrived(("ag2", g, h))
        t = dd.at[h, :, pl.ds(lo, hi - lo), mine]
        state["dc", g, h] = [send(t, t, dev(dc=1))]

    def turn(p):
        ends = (0, 3, 7, 10, 14)
        basis_there(0, 2 * p + 2)

        @pl.loop(ends[p], ends[p + 1])
        def _(b):
            s = pl.ds(pl.multiple_of(b * 128, 128), 128)
            hi, lo = split(bt[s, :].T)
            bhi[:, s] = hi
            blo[:, s] = lo

    def split_direction(h, part_of):
        @pl.loop(0, 4)
        def _(n):
            @pl.loop(0, 4)
            def _(i):
                hi, lo = split(dd[h, n, part_of * 4 + i])
                s = pl.ds(pl.multiple_of(i * QJ, QJ), QJ)
                dhi[n, s, :] = hi
                dlo[n, s, :] = lo

    def product_two(h, part_of, n0, n1):
        rh = jnp.concatenate([dhi[n0], dhi[n1]], axis=1)
        rl = jnp.concatenate([dlo[n0], dlo[n1]], axis=1)
        k = slice(part_of * 2 * KJ, (part_of + 1) * 2 * KJ)

        @pl.loop(0, 2)
        def _(i):
            s = pl.ds(pl.multiple_of(i * (KI // 2), KI // 2), KI // 2)
            new = dot3(bhi[s, k], blo[s, k], rh, rl)
            if part_of:
                back[h, n0, s, :] += new[:, :HN]
                back[h, n1, s, :] += new[:, HN:]
            else:
                back[h, n0, s, :] = new[:, :HN]
                back[h, n1, s, :] = new[:, HN:]

    def directions_there(h, lo, hi):
        for g, (first, end) in enumerate(GROUPS):
            if lo <= first and end <= hi:
                arrived(("dc", g, h))

    def ya0(h):
        directions_there(h, 0, 4)
        split_direction(h, 0)
        product_two(h, 0, yo, yp)
        product_two(h, 0, ym, y)

    def y0(h):
        directions_there(h, 4, 8)
        split_direction(h, 1)
        product_two(h, 1, yo, yp)
        state["ya", h] = [
            send(back.at[h, yo, top], ya.at[h, 0], dev(dy=1)),
            send(back.at[h, yo, low], ya.at[h, 1], dev(dy=3)),
        ]

    def y0b(h):
        product_two(h, 1, ym, y)

    def y1(h):
        up, dn = state.pop(("ya", h))
        up.wait_recv()
        back[h, yp, top, :] += ya[h, 0]
        a = send(back.at[h, yp], yb.at[h, 0], dev(dy=1))
        dn.wait_recv()
        back[h, ym, low, :] += ya[h, 1]
        b = send(back.at[h, ym], yb.at[h, 1], dev(dy=3))
        state["yb", h] = [a, b]

    out_back_copies = []

    def y2(h):
        arrived(("yb", h))

        @pl.loop(0, KI // 128)
        def _(i):
            s = pl.ds(pl.multiple_of(i * 128, 128), 128)
            b = back[h, y, s, :] + yb[h, 0, s, :] + yb[h, 1, s, :]
            back[h, y, s, :] = b
            norm[1] += jnp.sum((b * b).reshape(16, 8, HN), axis=0)

        out_back_copies.append(local(back.at[h, y], out_back.at[:, pl.ds(h * HN, HN)]))

    order = (
        (plain,), (turn, 0), (gf, 0), (gs, 0), (gs2, 0), (s0, 0, 0), (bf, 0), (bf, 1), (s0, 1, 0), (turn, 1),
        (s1, 0, 0), (s1, 1, 0), (gf, 1), (gs, 1), (s2, 0, 0), (s2, 1, 0), (s3, 0, 0), (s4, 0, 0), (s5, 0, 0),
        (gs2, 1), (s0, 1, 1), (s0, 2, 0), (s6, 0, 0), (s3, 1, 0), (s0, 2, 1), (s1, 1, 1), (s7, 0, 0),
        (s1, 2, 0), (s0, 0, 1), (s1, 2, 1), (s2, 2, 0), (s2, 1, 1), (turn, 2), (s2, 2, 1), (s0, 3, 0),
        (s0, 4, 0), (s0, 4, 1), (s3, 2, 0), (s1, 3, 0), (s4, 1, 0), (s1, 4, 0), (s0, 3, 1), (s2, 3, 0),
        (s4, 2, 0), (s2, 4, 0), (s5, 1, 0), (s3, 1, 1), (s1, 3, 1), (s3, 3, 0), (s5, 2, 0), (s3, 4, 0),
        (s3, 2, 1), (s1, 4, 1), (turn, 3), (s6, 1, 0), (s2, 3, 1), (s4, 3, 0), (s1, 0, 1), (s4, 4, 0),
        (s4, 1, 1), (s2, 4, 1), (s6, 2, 0), (s7, 1, 0), (s5, 3, 0), (s4, 2, 1), (s3, 3, 1), (s5, 4, 0),
        (s2, 0, 1), (s5, 1, 1), (s3, 4, 1), (ya0, 0), (s6, 3, 0), (s7, 2, 0), (s6, 4, 0), (s4, 4, 1),
        (s4, 3, 1), (s3, 0, 1), (s6, 1, 1), (s7, 3, 0), (s4, 0, 1), (s7, 4, 0), (s5, 0, 1), (s5, 2, 1),
        (s5, 4, 1), (s7, 1, 1), (s5, 3, 1), (y0, 0), (s6, 0, 1), (y0b, 0), (s6, 2, 1), (s6, 3, 1), (s6, 4, 1),
        (s7, 0, 1), (s7, 2, 1), (y1, 0), (s7, 4, 1), (s7, 3, 1), (ya0, 1), (y0, 1), (y0b, 1), (y2, 0),
        (y1, 1), (y2, 1),
    )
    adams_left = 2 * len(GROUPS)
    out_rot, out_rot_own = [], []
    for stage, *step in order:
        stage(*step)
        if stage is s4:
            adams_left -= 1
            if adams_left == 0:
                for src, dst in ((m2, new_mom_rot), (v2, new_var_rot)):
                    out_rot.append(send(src.at[o], dst.at[:, mine], dev(dc=1)))
                    out_rot_own.append(local(src.at[c], dst.at[:, mine]))

    slot = 0
    for moves in norm_moves:
        copies = []
        for to in moves:
            copies.append((slot, send(norm, nrecv.at[slot], to)))
            slot += 1
        for _, copy in copies:
            started.pop()
            copy.wait()
        total = norm[...]
        for k, _ in copies:
            total += nrecv[k]
        norm[...] = total
    last = local(norm, out_norm)
    assert count[0] <= N_COPIES and count[1] <= 16

    for copy in started:
        copy.wait_send()
    for copy in out_rot:
        copy.wait_recv()
    for copy in out_rot_own + out_plain + out_back_copies:
        copy.wait()
    last.wait()


def finish(back, norm, *refs):
    sources, outs = (*refs[:4], back), (*refs[5:9], refs[4])
    held_rot, held, norm_v, in_sems, out_sems = refs[9:]
    norm_in = pltpu.make_async_copy(norm, norm_v, in_sems.at[10])
    norm_in.start()
    pieces = []
    for i in range(5):
        for h in range(2):
            if i < 2:
                src, dst, here = sources[i].at[h], outs[i].at[h], held_rot.at[i, h]
            else:
                s = pl.ds(h * KJ, KJ)
                src, dst, here = sources[i].at[s], outs[i].at[s], held.at[i - 2, h]
            pieces.append((pltpu.make_async_copy(src, here, in_sems.at[2 * i + h]),
                           pltpu.make_async_copy(here, dst, out_sems.at[2 * i + h])))
    for into, _ in pieces:
        into.start()
    norm_in.wait()
    graft = jnp.sqrt(jnp.sum(norm_v[0], keepdims=True))
    own = jnp.sqrt(jnp.sum(norm_v[1], keepdims=True))
    scale = graft / (own + 1e-06)
    for k, (into, out) in enumerate(pieces):
        into.wait()
        if k >= 8:
            held[2, k - 8] = held[2, k - 8] * scale
        out.start()
    for _, out in pieces:
        out.wait()


def per_device(grad, basis, mom_rot, var_rot, mom_plain, var_plain):
    plain = jax.ShapeDtypeStruct((KI, KN), F32)
    rot = jax.ShapeDtypeStruct((2, QJ, 2 * KN), F32)
    norms = jax.ShapeDtypeStruct((2, 8, HN), F32)
    scratch = [
        pltpu.VMEM((2, 4, KI, HN), F32),
        pltpu.VMEM((2, 4, KI, HN), BF16),
        pltpu.VMEM((2, 4, KI, HN), BF16),
        pltpu.VMEM((4 * KJ, KI), F32),
        pltpu.VMEM((KJ, KI), BF16),
        pltpu.VMEM((KJ, KI), BF16),
        pltpu.VMEM((KI, 4 * KJ), BF16),
        pltpu.VMEM((KI, 4 * KJ), BF16),
        pltpu.VMEM((2, 4, 8, QJ, HN), F32),
        pltpu.VMEM((2, 4, 8, CJ, HN), F32),
        pltpu.VMEM((2, 2, 8, CJ, HN), F32),
        pltpu.VMEM((2, 2, 8, CJ, HN), F32),
        pltpu.VMEM((2, 8, CJ, HN), F32),
        pltpu.VMEM((2, 8, CJ, HN), F32),
        pltpu.VMEM((2, 2, CJ, 2 * KN), F32),
        pltpu.VMEM((2, 2, CJ, 2 * KN), F32),
        pltpu.VMEM((2, 8, CJ, HN), F32),
        pltpu.VMEM((2, 4, 8, QJ, HN), F32),
        pltpu.VMEM((4, 2 * KJ, HN), BF16),
        pltpu.VMEM((4, 2 * KJ, HN), BF16),
        pltpu.VMEM((2, 4, KI, HN), F32),
        pltpu.VMEM((2, 2, KI // 2, HN), F32),
        pltpu.VMEM((2, 2, KI, HN), F32),
        pltpu.VMEM((KI, KN), F32),
        pltpu.VMEM((KI, KN), F32),
        pltpu.VMEM((2, 8, HN), F32),
        pltpu.VMEM((13, 2, 8, HN), F32),
        pltpu.SemaphoreType.DMA((N_COPIES,)),
        pltpu.SemaphoreType.DMA((N_COPIES,)),
        pltpu.SemaphoreType.DMA((16,)),
    ]
    anywhere = pl.BlockSpec(memory_space=pl.ANY)
    out = pl.pallas_call(
        kernel,
        out_shape=(plain, norms, rot, rot, plain, plain),
        in_specs=[anywhere] * 6,
        out_specs=[anywhere] * 6,
        scratch_shapes=scratch,
        compiler_params=pltpu.CompilerParams(
            collective_id=0, has_side_effects=True, vmem_limit_bytes=63 * 1024 * 1024
        ),
        cost_estimate=pl.CostEstimate(flops=20_000_000_000, bytes_accessed=12_000_000, transcendentals=0),
    )(grad, basis.T, mom_rot.reshape(2, QJ, 2 * KN), var_rot.reshape(2, QJ, 2 * KN), mom_plain, var_plain)
    update, new_mom_rot, new_var_rot, new_mom_plain, new_var_plain = pl.pallas_call(
        finish,
        out_shape=(plain, rot, rot, plain, plain),
        in_specs=[anywhere] * 6,
        out_specs=[anywhere] * 5,
        scratch_shapes=[
            pltpu.VMEM((2, 2, QJ, 2 * KN), F32),
            pltpu.VMEM((3, 2, KJ, KN), F32),
            pltpu.VMEM((2, 8, HN), F32),
            pltpu.SemaphoreType.DMA((11,)),
            pltpu.SemaphoreType.DMA((10,)),
        ],
        compiler_params=pltpu.CompilerParams(vmem_limit_bytes=60 * 1024 * 1024),
        cost_estimate=pl.CostEstimate(flops=1_000_000, bytes_accessed=9_000_000, transcendentals=0),
    )(*out)
    return (
        update,
        new_mom_rot.reshape(KJ, 2 * KN),
        new_var_rot.reshape(KJ, 2 * KN),
        new_mom_plain,
        new_var_plain,
    )


def solution(mesh):
    return jax.shard_map(
        per_device,
        mesh=mesh,
        in_specs=(
            P("rows", "cols"),
            P("rows", "cols"),
            P("cols", "rows"),
            P("cols", "rows"),
            P("rows", "cols"),
            P("rows", "cols"),
        ),
        out_specs=(
            P("rows", "cols"),
            P("cols", "rows"),
            P("cols", "rows"),
            P("rows", "cols"),
            P("rows", "cols"),
        ),
        check_vma=False,
    )
```

time: 456 us -> 151 us (0.33)
  waiting for transfers between devices: 305 us -> 0 us
  Pallas kernels: 0 us -> 150 us
  blocking collectives: 64.3 us -> 0 us
  matrix products: 57.9 us -> 0 us
  between operations: 15.1 us -> 0.8 us
  other arithmetic: 9.92 us -> 0 us
    all_gather x2 -> x0, waiting for transfers between devices: 160 us -> none  [the longest x1 115 us: per_device(): lax.all_gather(grad, 'cols', axis=1, tiled=True)]
    pallas_call x0 -> x2, Pallas kernels: none -> 150 us  [the longest x1 146 us: per_device(): pl.pallas_call(kernel, out_shape=(plain, norms, rot, rot, plain, plain),...]
    reduce_scatter x2 -> x0, waiting for transfers between devices: 144 us -> none  [the longest x1 97.2 us: per_device(): lax.psum_scatter(partial_back, 'cols', scatter_dimension=1, tiled=True)]
    psum x1 -> x0, blocking collectives: 64.3 us -> none  [per_device(): graft_total = lax.psum(plain_local, ('rows', 'cols'))]
    dot_general x2 -> x0, matrix products: 57.9 us -> none  [the longest x1 30.5 us: per_device(): jnp.dot(basis, lax.all_gather(direction, 'rows', axis=1, tiled=True), pre...]
    reduce_sum x2 -> x0, other arithmetic: 5.6 us -> none  [the longest x1 3.59 us: per_device(): plain_local = jnp.sum(plain * plain)]
  transfers between devices with their start and end apart: 4 -> 0, of which waited for: 4 -> 0; matrix products, arithmetic and copies ran while one was open for 1% -> 0% of each run, Pallas kernels for 0% -> 0%
where the time goes in v2:
time: 151 us
  Pallas kernels  150 us (99%)
    pallas_call x1, Pallas kernels, per_device(): pl.pallas_call(kernel, out_shape=(plain, norms, rot, rot, plain, plain),...  146 us
    pallas_call x1, Pallas kernels, per_device(): pl.pallas_call(finish, out_shape=(plain, rot, rot, plain, plain), in_spec...  4.12 us

profile of v2, /device:TPU:0, one launch (start us, length us, event | category | flops | bytes accessed | tf_op | source)
XLA Modules:
  0.0 150.9 jit_solution(585659091689005960)
XLA Ops:
  0.6 146.0 %shard_map.101 = (f32[896,256]{1,0:T(8,128)}, f32[2,8,128]{2,1,0:T(8,128)}, f32[2,224,512]{2,1,0:T(8,128)}, f32[2,224,512]{2,1,0:T(8,128)}, f32[896,256]{1,0:T(8,128)}, /*index=5*/f32[896,256]{1,0:T(8,128)}) custom-call(f32[896,256]{1,0:T(8,128)} %grad.1, f32[448,896]{1,0:T(8,128)} %bitcast.5, f32[2,224,512]{2,1,0:T(8,128)} %bitcast.6, ...), custom_call_target="tpu_custom_call" | custom-call | flops 20000000000 | bytes 12000000 | tf_op jit(solution)/shard_map/pallas_call | solution.py:512
  146.6 4.1 %shard_map.102 = (f32[896,256]{1,0:T(8,128)}, f32[2,224,512]{2,1,0:T(8,128)}, f32[2,224,512]{2,1,0:T(8,128)}, f32[896,256]{1,0:T(8,128)}, f32[896,256]{1,0:T(8,128)}) custom-call(f32[896,256]{1,0:T(8,128)} %get-tuple-element.16.back, f32[2,8,128]{2,1,0:T(8,128)} %get-tuple-element.17.norm, f32[2,224,512]{2,1,0:T(8,128)} %get-tuple-element.18.refs_0_, ...), custom_call_target="tpu_custom_call" | custom-call | flops 1000000 | bytes 9000000 | tf_op jit(solution)/shard_map/pallas_call | solution.py:523

commit v3 on v2

--- a/solution.py
+++ b/solution.py
@@ -23,7 +23,7 @@
 CJ = QJ // 2
 CHUNKS = ((0, 0), (0, 1), (1, 1), (3, 0), (1, 0), (3, 1), (2, 0), (2, 1))
 GROUPS = ((0, 2), (2, 4), (4, 6), (6, 7), (7, 8))
-N_COPIES = 176
+N_COPIES = 192
 
 
 def adam(moment, second, values):
@@ -40,8 +40,9 @@
 
 
 def dot3(lh, ll, rh, rl):
-    dot = functools.partial(jnp.dot, preferred_element_type=F32)
-    return dot(lh, rh) + (dot(lh, rl) + dot(ll, rh))
+    left = jnp.concatenate([lh, lh, ll], axis=1)
+    right = jnp.concatenate([rh, rl, rh], axis=0)
+    return jnp.dot(left, right, preferred_element_type=F32)
 
 
 def kernel(
@@ -109,11 +110,13 @@
     def chunk(i):
         return bt.at[pl.ds(i * QJ, QJ)]
 
-    def gather_grad(h):
-        own = grad.at[:, pl.ds(h * HN, HN)]
-        state["g", h] = [send(own, gg.at[h, y], dev(dy=1)), send(own, gg.at[h, y], dev(dy=3))]
-
-    gather_grad(0)
+    def gg_send(h):
+        lanes = pl.ds(h * HN, HN)
+        for way, first, second in ((1, top, low), (3, low, top)):
+            state["g", h, way] = [send(grad.at[first, lanes], gg.at[h, y, first], dev(dy=way))]
+            state["g_rest", h, way] = [send(grad.at[second, lanes], gg.at[h, y, second], dev(dy=way))]
+
+    gg_send(0)
     halves = [basis_t.at[pl.ds(q * QJ, QJ)] for q in range(2)]
     state["b", 3] = [send(halves[0], chunk(3), dev(dz=1))]
     state["b", 2] = [send(halves[1], chunk(2), dev(dz=3))]
@@ -158,17 +161,16 @@
             glo[h, n, s, :] = lo
 
     def gf(h):
-        up, dn = state.pop(("g", h))
-        up.wait_recv()
+        arrived(("g", h, 1))
         a = send(gg.at[h, ym, top], gg.at[h, ym, top], dev(dy=1))
-        dn.wait_recv()
+        arrived(("g", h, 3))
         b = send(gg.at[h, yp, low], gg.at[h, yp, low], dev(dy=3))
         state["g2", h] = [a, b]
-        if h == 0:
-            gather_grad(1)
 
     def gs(h):
         done(own_g)
+        arrived(("g_rest", h, 1))
+        arrived(("g_rest", h, 3))
         for n in (y, ym, yp):
             split_grad(h, n)
 
@@ -217,14 +219,12 @@
         lhi[:size, :] = high
         llo[:size, :] = rest
 
-        @pl.loop(0, 2)
-        def _(p):
-            rh = jnp.concatenate([ghi[h, 2 * p], ghi[h, 2 * p + 1]], axis=1)
-            rl = jnp.concatenate([glo[h, 2 * p], glo[h, 2 * p + 1]], axis=1)
-            new = dot3(lhi[:size, :], llo[:size, :], rh, rl)
+        rh = jnp.concatenate([ghi[h, n] for n in range(4)], axis=1)
+        rl = jnp.concatenate([glo[h, n] for n in range(4)], axis=1)
+        new = dot3(lhi[:size, :], llo[:size, :], rh, rl)
+        for n in range(4):
             for i in range(hi - lo):
-                part[h, 2 * p, lo + i] = new[i * QJ:(i + 1) * QJ, :HN]
-                part[h, 2 * p + 1, lo + i] = new[i * QJ:(i + 1) * QJ, HN:]
+                part[h, n, lo + i] = new[i * QJ:(i + 1) * QJ, n * HN:(n + 1) * HN]
 
         group = pl.ds(lo, hi - lo)
         state["x", g, h] = [send(part.at[h, :, group, other], rx.at[h, :, group], dev(dc=1))]
@@ -328,21 +328,14 @@
                 dhi[n, s, :] = hi
                 dlo[n, s, :] = lo
 
-    def product_two(h, part_of, n0, n1):
-        rh = jnp.concatenate([dhi[n0], dhi[n1]], axis=1)
-        rl = jnp.concatenate([dlo[n0], dlo[n1]], axis=1)
+    def product_two(h, part_of, s):
+        rh = jnp.concatenate([dhi[n] for n in range(4)], axis=1)
+        rl = jnp.concatenate([dlo[n] for n in range(4)], axis=1)
         k = slice(part_of * 2 * KJ, (part_of + 1) * 2 * KJ)
-
-        @pl.loop(0, 2)
-        def _(i):
-            s = pl.ds(pl.multiple_of(i * (KI // 2), KI // 2), KI // 2)
-            new = dot3(bhi[s, k], blo[s, k], rh, rl)
-            if part_of:
-                back[h, n0, s, :] += new[:, :HN]
-                back[h, n1, s, :] += new[:, HN:]
-            else:
-                back[h, n0, s, :] = new[:, :HN]
-                back[h, n1, s, :] = new[:, HN:]
+        new = dot3(bhi[s, k], blo[s, k], rh, rl)
+        for n in range(4):
+            tile = new[:, n * HN:(n + 1) * HN]
+            back[h, n, s, :] = back[h, n, s, :] + tile if part_of else tile
 
     def directions_there(h, lo, hi):
         for g, (first, end) in enumerate(GROUPS):
@@ -352,30 +345,29 @@
     def ya0(h):
         directions_there(h, 0, 4)
         split_direction(h, 0)
-        product_two(h, 0, yo, yp)
-        product_two(h, 0, ym, y)
+        product_two(h, 0, top)
+        product_two(h, 0, low)
 
     def y0(h):
         directions_there(h, 4, 8)
         split_direction(h, 1)
-        product_two(h, 1, yo, yp)
-        state["ya", h] = [
-            send(back.at[h, yo, top], ya.at[h, 0], dev(dy=1)),
-            send(back.at[h, yo, low], ya.at[h, 1], dev(dy=3)),
-        ]
+        product_two(h, 1, top)
+        state["ya", h] = [send(back.at[h, yo, top], ya.at[h, 0], dev(dy=1))]
+        state["yb", h] = [send(back.at[h, ym, top], yb.at[h, 1, top], dev(dy=3))]
 
     def y0b(h):
-        product_two(h, 1, ym, y)
+        product_two(h, 1, low)
+        state["ya", h].append(send(back.at[h, yo, low], ya.at[h, 1], dev(dy=3)))
+        state["yb", h].append(send(back.at[h, yp, low], yb.at[h, 0, low], dev(dy=1)))
 
     def y1(h):
         up, dn = state.pop(("ya", h))
         up.wait_recv()
         back[h, yp, top, :] += ya[h, 0]
-        a = send(back.at[h, yp], yb.at[h, 0], dev(dy=1))
+        state["yb", h].append(send(back.at[h, yp, top], yb.at[h, 0, top], dev(dy=1)))
         dn.wait_recv()
         back[h, ym, low, :] += ya[h, 1]
-        b = send(back.at[h, ym], yb.at[h, 1], dev(dy=3))
-        state["yb", h] = [a, b]
+        state["yb", h].append(send(back.at[h, ym, low], yb.at[h, 1, low], dev(dy=3)))
 
     out_back_copies = []
 
@@ -392,19 +384,19 @@
         out_back_copies.append(local(back.at[h, y], out_back.at[:, pl.ds(h * HN, HN)]))
 
     order = (
-        (plain,), (turn, 0), (gf, 0), (gs, 0), (gs2, 0), (s0, 0, 0), (bf, 0), (bf, 1), (s0, 1, 0), (turn, 1),
-        (s1, 0, 0), (s1, 1, 0), (gf, 1), (gs, 1), (s2, 0, 0), (s2, 1, 0), (s3, 0, 0), (s4, 0, 0), (s5, 0, 0),
-        (gs2, 1), (s0, 1, 1), (s0, 2, 0), (s6, 0, 0), (s3, 1, 0), (s0, 2, 1), (s1, 1, 1), (s7, 0, 0),
-        (s1, 2, 0), (s0, 0, 1), (s1, 2, 1), (s2, 2, 0), (s2, 1, 1), (turn, 2), (s2, 2, 1), (s0, 3, 0),
-        (s0, 4, 0), (s0, 4, 1), (s3, 2, 0), (s1, 3, 0), (s4, 1, 0), (s1, 4, 0), (s0, 3, 1), (s2, 3, 0),
-        (s4, 2, 0), (s2, 4, 0), (s5, 1, 0), (s3, 1, 1), (s1, 3, 1), (s3, 3, 0), (s5, 2, 0), (s3, 4, 0),
-        (s3, 2, 1), (s1, 4, 1), (turn, 3), (s6, 1, 0), (s2, 3, 1), (s4, 3, 0), (s1, 0, 1), (s4, 4, 0),
-        (s4, 1, 1), (s2, 4, 1), (s6, 2, 0), (s7, 1, 0), (s5, 3, 0), (s4, 2, 1), (s3, 3, 1), (s5, 4, 0),
-        (s2, 0, 1), (s5, 1, 1), (s3, 4, 1), (ya0, 0), (s6, 3, 0), (s7, 2, 0), (s6, 4, 0), (s4, 4, 1),
-        (s4, 3, 1), (s3, 0, 1), (s6, 1, 1), (s7, 3, 0), (s4, 0, 1), (s7, 4, 0), (s5, 0, 1), (s5, 2, 1),
-        (s5, 4, 1), (s7, 1, 1), (s5, 3, 1), (y0, 0), (s6, 0, 1), (y0b, 0), (s6, 2, 1), (s6, 3, 1), (s6, 4, 1),
-        (s7, 0, 1), (s7, 2, 1), (y1, 0), (s7, 4, 1), (s7, 3, 1), (ya0, 1), (y0, 1), (y0b, 1), (y2, 0),
-        (y1, 1), (y2, 1),
+        (turn, 0), (plain,), (gf, 0), (gs, 0), (gg_send, 1), (gs2, 0), (s0, 0, 0), (s0, 1, 0), (gf, 1),
+        (s1, 0, 0), (bf, 0), (turn, 1), (s2, 0, 0), (s1, 1, 0), (gs, 1), (bf, 1), (gs2, 1), (s0, 1, 1),
+        (s0, 0, 1), (s2, 1, 0), (s3, 0, 0), (s4, 0, 0), (s5, 0, 0), (s1, 1, 1), (s0, 2, 0), (s1, 0, 1),
+        (s0, 2, 1), (s2, 1, 1), (s1, 2, 0), (s2, 0, 1), (s3, 1, 0), (turn, 2), (s1, 2, 1), (s2, 2, 0),
+        (s6, 0, 0), (s3, 1, 1), (s0, 4, 0), (s2, 2, 1), (s0, 3, 0), (s0, 3, 1), (s1, 4, 0), (s3, 2, 0),
+        (s0, 4, 1), (s1, 3, 0), (s4, 1, 0), (s2, 4, 0), (s1, 3, 1), (s3, 2, 1), (s2, 3, 0), (s4, 2, 0),
+        (s1, 4, 1), (s5, 1, 0), (s3, 4, 0), (s3, 0, 1), (s2, 3, 1), (s3, 3, 0), (s7, 0, 0), (s5, 2, 0),
+        (s4, 4, 0), (turn, 3), (s6, 1, 0), (s4, 3, 0), (s3, 3, 1), (s2, 4, 1), (s4, 0, 1), (s4, 2, 1),
+        (s5, 4, 0), (s4, 1, 1), (s5, 3, 0), (s7, 1, 0), (s3, 4, 1), (s6, 2, 0), (s4, 3, 1), (s6, 4, 0),
+        (s6, 3, 0), (s5, 0, 1), (s5, 2, 1), (s7, 2, 0), (s5, 1, 1), (s7, 4, 0), (s4, 4, 1), (s7, 3, 0),
+        (ya0, 0), (s6, 0, 1), (s5, 4, 1), (y0, 0), (s6, 1, 1), (s7, 0, 1), (s5, 3, 1), (s6, 2, 1), (y0b, 0),
+        (s7, 1, 1), (s6, 4, 1), (s6, 3, 1), (s7, 2, 1), (s7, 4, 1), (y1, 0), (s7, 3, 1), (ya0, 1), (y0, 1),
+        (y0b, 1), (y1, 1), (y2, 0), (y2, 1),
     )
     adams_left = 2 * len(GROUPS)
     out_rot, out_rot_own = [], []

time: 151 us -> 147 us (0.974)
  Pallas kernels: 150 us -> 146 us
    pallas_call x1, Pallas kernels: 146 us -> 142 us  [per_device(): pl.pallas_call(kernel, out_shape=(plain, norms, rot, rot, plain, plain),...]
where the time goes in v3:
time: 147 us
  Pallas kernels  146 us (99%)
    pallas_call x1, Pallas kernels, per_device(): pl.pallas_call(kernel, out_shape=(plain, norms, rot, rot, plain, plain),...  142 us
    pallas_call x1, Pallas kernels, per_device(): pl.pallas_call(finish, out_shape=(plain, rot, rot, plain, plain), in_spec...  4.12 us

profile of v3, /device:TPU:0, one launch (start us, length us, event | category | flops | bytes accessed | tf_op | source)
XLA Modules:
  0.0 146.9 jit_solution(8879558569933646709)
XLA Ops:
  0.6 142.0 %shard_map.101 = (f32[896,256]{1,0:T(8,128)}, f32[2,8,128]{2,1,0:T(8,128)}, f32[2,224,512]{2,1,0:T(8,128)}, f32[2,224,512]{2,1,0:T(8,128)}, f32[896,256]{1,0:T(8,128)}, /*index=5*/f32[896,256]{1,0:T(8,128)}) custom-call(f32[896,256]{1,0:T(8,128)} %grad.1, f32[448,896]{1,0:T(8,128)} %bitcast.5, f32[2,224,512]{2,1,0:T(8,128)} %bitcast.6, ...), custom_call_target="tpu_custom_call" | custom-call | flops 20000000000 | bytes 12000000 | tf_op jit(solution)/shard_map/pallas_call | solution.py:504
  142.6 4.1 %shard_map.102 = (f32[896,256]{1,0:T(8,128)}, f32[2,224,512]{2,1,0:T(8,128)}, f32[2,224,512]{2,1,0:T(8,128)}, f32[896,256]{1,0:T(8,128)}, f32[896,256]{1,0:T(8,128)}) custom-call(f32[896,256]{1,0:T(8,128)} %get-tuple-element.16.back, f32[2,8,128]{2,1,0:T(8,128)} %get-tuple-element.17.norm, f32[2,224,512]{2,1,0:T(8,128)} %get-tuple-element.18.refs_0_, ...), custom_call_target="tpu_custom_call" | custom-call | flops 1000000 | bytes 9000000 | tf_op jit(solution)/shard_map/pallas_call | solution.py:515

commit v4 on v3

--- a/solution.py
+++ b/solution.py
@@ -22,8 +22,8 @@
 HN = KN // 2
 CJ = QJ // 2
 CHUNKS = ((0, 0), (0, 1), (1, 1), (3, 0), (1, 0), (3, 1), (2, 0), (2, 1))
-GROUPS = ((0, 2), (2, 4), (4, 6), (6, 7), (7, 8))
-N_COPIES = 192
+GROUPS = ((0, 2), (2, 4), (4, 5), (5, 6), (6, 7), (7, 8))
+N_COPIES = 224
 
 
 def adam(moment, second, values):
@@ -120,8 +120,6 @@
     halves = [basis_t.at[pl.ds(q * QJ, QJ)] for q in range(2)]
     state["b", 3] = [send(halves[0], chunk(3), dev(dz=1))]
     state["b", 2] = [send(halves[1], chunk(2), dev(dz=3))]
-    state["b", 5] = [send(halves[1], chunk(5), dev(dz=1))]
-    state["b", 4] = [send(halves[0], chunk(4), dev(dz=3))]
     own_g = [local(grad.at[:, pl.ds(h * HN, HN)], gg.at[h, y]) for h in range(2)]
     own_b = [local(basis_t, bt.at[pl.ds(0, KJ)])]
     own_plain = [local(mom_plain, mp), local(var_plain, vp)]
@@ -185,6 +183,12 @@
         else:
             arrived(("b", 2))
             state["b", 7] = [send(chunk(2), chunk(7), dev(dz=3))]
+
+    def bo(way):
+        if way == 0:
+            state["b", 5] = [send(halves[1], chunk(5), dev(dz=1))]
+        else:
+            state["b", 4] = [send(halves[0], chunk(4), dev(dz=3))]
 
     def basis_there(lo, hi):
         for i in range(lo, hi):
@@ -279,33 +283,38 @@
             v2[half, q, :, lanes] = v
             if off:
                 direc[h, i] = d
-                state["d", i, h] = [send(direc.at[h, i], dd.at[h, x, i, mine], dev(dz=4 - off))]
+                state["d", i, h] = [send(direc.at[h, i], dd.at[h, 0, i, mine], dev(dz=4 - off))]
             else:
-                dd[h, x, i, mine, :] = d
+                dd[h, 0, i, mine, :] = d
 
     def s5(g, h):
         lo, hi = GROUPS[g]
+        group = pl.ds(lo, hi - lo)
         for i in away(g):
             arrived(("d", i, h))
-        t = dd.at[h, x, pl.ds(lo, hi - lo), mine]
-        state["ag", g, h] = [send(t, t, dev(dx=1)), send(t, t, dev(dx=3))]
+        t = dd.at[h, 0, group, mine]
+        state["ag", g, h] = [
+            send(t, dd.at[h, 2, group, mine], dev(dx=1)),
+            send(t, dd.at[h, 1, group, mine], dev(dx=3)),
+        ]
 
     def s6(g, h):
+        lo, hi = GROUPS[g]
         (first, up), (second, dn) = ways(g)
         a, b = state.pop(("ag", g, h))
         a.wait_recv()
-        t = dd.at[h, xm, first, up]
-        a = send(t, t, dev(dx=1))
+        a = send(dd.at[h, 2, first, up], dd.at[h, 3, first, up], dev(dx=1))
         b.wait_recv()
-        t = dd.at[h, xp, second, dn]
-        b = send(t, t, dev(dx=3))
+        b = send(dd.at[h, 1, second, dn], dd.at[h, 3, second, dn], dev(dx=3))
         state["ag2", g, h] = [a, b]
+        t = dd.at[h, pl.ds(0, 3), pl.ds(lo, hi - lo), mine]
+        state["dc", g, h] = [send(t, t, dev(dc=1))]
 
     def s7(g, h):
         lo, hi = GROUPS[g]
         arrived(("ag2", g, h))
-        t = dd.at[h, :, pl.ds(lo, hi - lo), mine]
-        state["dc", g, h] = [send(t, t, dev(dc=1))]
+        t = dd.at[h, 3, pl.ds(lo, hi - lo), mine]
+        state["dc", g, h].append(send(t, t, dev(dc=1)))
 
     def turn(p):
         ends = (0, 3, 7, 10, 14)
@@ -321,9 +330,12 @@
     def split_direction(h, part_of):
         @pl.loop(0, 4)
         def _(n):
+            d = (n + 4 - x) % 4
+            place = d + d // 2 * (1 - 2 * (d % 2))
+
             @pl.loop(0, 4)
             def _(i):
-                hi, lo = split(dd[h, n, part_of * 4 + i])
+                hi, lo = split(dd[h, place, part_of * 4 + i])
                 s = pl.ds(pl.multiple_of(i * QJ, QJ), QJ)
                 dhi[n, s, :] = hi
                 dlo[n, s, :] = lo
@@ -384,19 +396,21 @@
         out_back_copies.append(local(back.at[h, y], out_back.at[:, pl.ds(h * HN, HN)]))
 
     order = (
-        (turn, 0), (plain,), (gf, 0), (gs, 0), (gg_send, 1), (gs2, 0), (s0, 0, 0), (s0, 1, 0), (gf, 1),
-        (s1, 0, 0), (bf, 0), (turn, 1), (s2, 0, 0), (s1, 1, 0), (gs, 1), (bf, 1), (gs2, 1), (s0, 1, 1),
-        (s0, 0, 1), (s2, 1, 0), (s3, 0, 0), (s4, 0, 0), (s5, 0, 0), (s1, 1, 1), (s0, 2, 0), (s1, 0, 1),
-        (s0, 2, 1), (s2, 1, 1), (s1, 2, 0), (s2, 0, 1), (s3, 1, 0), (turn, 2), (s1, 2, 1), (s2, 2, 0),
-        (s6, 0, 0), (s3, 1, 1), (s0, 4, 0), (s2, 2, 1), (s0, 3, 0), (s0, 3, 1), (s1, 4, 0), (s3, 2, 0),
-        (s0, 4, 1), (s1, 3, 0), (s4, 1, 0), (s2, 4, 0), (s1, 3, 1), (s3, 2, 1), (s2, 3, 0), (s4, 2, 0),
-        (s1, 4, 1), (s5, 1, 0), (s3, 4, 0), (s3, 0, 1), (s2, 3, 1), (s3, 3, 0), (s7, 0, 0), (s5, 2, 0),
-        (s4, 4, 0), (turn, 3), (s6, 1, 0), (s4, 3, 0), (s3, 3, 1), (s2, 4, 1), (s4, 0, 1), (s4, 2, 1),
-        (s5, 4, 0), (s4, 1, 1), (s5, 3, 0), (s7, 1, 0), (s3, 4, 1), (s6, 2, 0), (s4, 3, 1), (s6, 4, 0),
-        (s6, 3, 0), (s5, 0, 1), (s5, 2, 1), (s7, 2, 0), (s5, 1, 1), (s7, 4, 0), (s4, 4, 1), (s7, 3, 0),
-        (ya0, 0), (s6, 0, 1), (s5, 4, 1), (y0, 0), (s6, 1, 1), (s7, 0, 1), (s5, 3, 1), (s6, 2, 1), (y0b, 0),
-        (s7, 1, 1), (s6, 4, 1), (s6, 3, 1), (s7, 2, 1), (s7, 4, 1), (y1, 0), (s7, 3, 1), (ya0, 1), (y0, 1),
-        (y0b, 1), (y1, 1), (y2, 0), (y2, 1),
+        (turn, 0), (gf, 0), (gs, 0), (bo, 1), (bo, 0), (plain,), (gg_send, 1), (gs2, 0), (s0, 0, 0),
+        (s1, 0, 0), (s0, 1, 0), (gf, 1), (s2, 0, 0), (turn, 1), (bf, 1), (gs, 1), (s3, 0, 0), (s4, 0, 0),
+        (s1, 1, 0), (s5, 0, 0), (gs2, 1), (bf, 0), (s0, 1, 1), (s2, 1, 0), (s0, 3, 0), (s0, 0, 1), (s1, 3, 0),
+        (s1, 1, 1), (s6, 0, 0), (s0, 3, 1), (s2, 3, 0), (s1, 0, 1), (s0, 2, 1), (s2, 1, 1), (s0, 2, 0),
+        (s1, 3, 1), (s1, 2, 1), (turn, 2), (s3, 3, 0), (s1, 2, 0), (s7, 0, 0), (s2, 3, 1), (s2, 2, 1),
+        (s2, 0, 1), (s2, 2, 0), (s3, 1, 1), (s3, 1, 0), (s0, 4, 0), (s4, 3, 0), (s0, 5, 0), (s3, 2, 1),
+        (s1, 4, 0), (s3, 2, 0), (s5, 3, 0), (s4, 1, 0), (s1, 5, 0), (s2, 4, 0), (s0, 5, 1), (s6, 3, 0),
+        (s2, 5, 0), (s4, 2, 0), (s5, 1, 0), (s3, 4, 0), (s3, 0, 1), (s0, 4, 1), (s3, 5, 0), (s1, 5, 1),
+        (s5, 2, 0), (s7, 3, 0), (s3, 3, 1), (s4, 4, 0), (s1, 4, 1), (s6, 1, 0), (s4, 2, 1), (s2, 5, 1),
+        (s4, 5, 0), (s4, 0, 1), (s6, 2, 0), (s4, 1, 1), (s5, 4, 0), (turn, 3), (s4, 3, 1), (s5, 5, 0),
+        (s7, 1, 0), (s3, 5, 1), (s5, 1, 1), (s2, 4, 1), (s6, 4, 0), (s7, 2, 0), (s6, 5, 0), (s5, 0, 1),
+        (ya0, 0), (s7, 4, 0), (s7, 5, 0), (s4, 5, 1), (s5, 3, 1), (s3, 4, 1), (s6, 1, 1), (y0, 0), (s6, 0, 1),
+        (s7, 1, 1), (s5, 2, 1), (s4, 4, 1), (s5, 5, 1), (y0b, 0), (s7, 0, 1), (s6, 3, 1), (s5, 4, 1),
+        (s6, 2, 1), (s6, 5, 1), (ya0, 1), (s6, 4, 1), (s7, 5, 1), (y1, 0), (s7, 3, 1), (s7, 2, 1), (s7, 4, 1),
+        (y0, 1), (y2, 0), (y0b, 1), (y1, 1), (y2, 1),
     )
     adams_left = 2 * len(GROUPS)
     out_rot, out_rot_own = [], []

time: 147 us -> 151 us (1.027)
  Pallas kernels: 146 us -> 150 us
    pallas_call x1, Pallas kernels: 142 us -> 146 us  [per_device(): pl.pallas_call(kernel, out_shape=(plain, norms, rot, rot, plain, plain),...]
where the time goes in v4:
time: 151 us
  Pallas kernels  150 us (99%)
    pallas_call x1, Pallas kernels, per_device(): pl.pallas_call(kernel, out_shape=(plain, norms, rot, rot, plain, plain),...  146 us
    pallas_call x1, Pallas kernels, per_device(): pl.pallas_call(finish, out_shape=(plain, rot, rot, plain, plain), in_spec...  4.12 us

profile of v4, /device:TPU:0, one launch (start us, length us, event | category | flops | bytes accessed | tf_op | source)
XLA Modules:
  0.0 150.5 jit_solution(15945642961268696480)
XLA Ops:
  0.6 145.6 %shard_map.101 = (f32[896,256]{1,0:T(8,128)}, f32[2,8,128]{2,1,0:T(8,128)}, f32[2,224,512]{2,1,0:T(8,128)}, f32[2,224,512]{2,1,0:T(8,128)}, f32[896,256]{1,0:T(8,128)}, /*index=5*/f32[896,256]{1,0:T(8,128)}) custom-call(f32[896,256]{1,0:T(8,128)} %grad.1, f32[448,896]{1,0:T(8,128)} %bitcast.5, f32[2,224,512]{2,1,0:T(8,128)} %bitcast.6, ...), custom_call_target="tpu_custom_call" | custom-call | flops 20000000000 | bytes 12000000 | tf_op jit(solution)/shard_map/pallas_call | solution.py:518
  146.3 4.1 %shard_map.102 = (f32[896,256]{1,0:T(8,128)}, f32[2,224,512]{2,1,0:T(8,128)}, f32[2,224,512]{2,1,0:T(8,128)}, f32[896,256]{1,0:T(8,128)}, f32[896,256]{1,0:T(8,128)}) custom-call(f32[896,256]{1,0:T(8,128)} %get-tuple-element.16.back, f32[2,8,128]{2,1,0:T(8,128)} %get-tuple-element.17.norm, f32[2,224,512]{2,1,0:T(8,128)} %get-tuple-element.18.refs_0_, ...), custom_call_target="tpu_custom_call" | custom-call | flops 1000000 | bytes 9000000 | tf_op jit(solution)/shard_map/pallas_call | solution.py:529

commit v5 on v3

--- a/solution.py
+++ b/solution.py
@@ -1,4 +1,4 @@
-import functools
+import math
 
 import jax
 import jax.numpy as jnp
@@ -23,7 +23,7 @@
 CJ = QJ // 2
 CHUNKS = ((0, 0), (0, 1), (1, 1), (3, 0), (1, 0), (3, 1), (2, 0), (2, 1))
 GROUPS = ((0, 2), (2, 4), (4, 6), (6, 7), (7, 8))
-N_COPIES = 192
+N_COPIES = 128
 
 
 def adam(moment, second, values):
@@ -80,19 +80,35 @@
         pl.semaphore_signal(barrier, inc=1, device_id=p, device_id_type=pl.DeviceIdType.MESH)
     pl.semaphore_wait(barrier, len(partners))
 
-    count = [0, 0]
-    started = []
-
-    def send(src, dst, to):
-        i = count[0]
+    kinds, sizes, count = [], {}, [0, 0]
+
+    def new_slot():
         count[0] += 1
+        return count[0] - 1
+
+    def send(src, dst, to, kind, slot=None):
+        if kind not in kinds:
+            kinds.append(kind)
+            sizes[kind] = 0
+        sizes[kind] += math.prod(src.shape)
         copy = pltpu.make_async_remote_copy(
-            src_ref=src, dst_ref=dst, send_sem=ssem.at[i], recv_sem=rsem.at[i],
+            src_ref=src, dst_ref=dst, send_sem=ssem.at[kinds.index(kind)],
+            recv_sem=rsem.at[new_slot() if slot is None else slot],
             device_id=to, device_id_type=pl.DeviceIdType.MESH,
         )
         copy.start()
-        started.append(copy)
         return copy
+
+    def whole(ref, slot, kind=0):
+        return pltpu.make_async_remote_copy(
+            src_ref=ref, dst_ref=ref, send_sem=ssem.at[kind], recv_sem=rsem.at[slot],
+            device_id=dev(dc=1), device_id_type=pl.DeviceIdType.MESH,
+        )
+
+    def sent(kind, *refs):
+        assert sizes.pop(kind) == sum(math.prod(ref.shape) for ref in refs)
+        for ref in refs:
+            whole(ref, 0, kinds.index(kind)).wait_send()
 
     def local(src, dst):
         i = count[1]
@@ -112,23 +128,25 @@
 
     def gg_send(h):
         lanes = pl.ds(h * HN, HN)
+        rest = new_slot()
         for way, first, second in ((1, top, low), (3, low, top)):
-            state["g", h, way] = [send(grad.at[first, lanes], gg.at[h, y, first], dev(dy=way))]
-            state["g_rest", h, way] = [send(grad.at[second, lanes], gg.at[h, y, second], dev(dy=way))]
+            state["g", h, way] = [send(grad.at[first, lanes], gg.at[h, y, first], dev(dy=way), "g")]
+            send(grad.at[second, lanes], gg.at[h, y, second], dev(dy=way), "g", rest)
+        state["g_rest", h] = [whole(gg.at[h, y], rest)]
 
     gg_send(0)
     halves = [basis_t.at[pl.ds(q * QJ, QJ)] for q in range(2)]
-    state["b", 3] = [send(halves[0], chunk(3), dev(dz=1))]
-    state["b", 2] = [send(halves[1], chunk(2), dev(dz=3))]
-    state["b", 5] = [send(halves[1], chunk(5), dev(dz=1))]
-    state["b", 4] = [send(halves[0], chunk(4), dev(dz=3))]
+    state["b", 3] = [send(halves[0], chunk(3), dev(dz=1), "b")]
+    state["b", 2] = [send(halves[1], chunk(2), dev(dz=3), "b")]
+    state["b", 5] = [send(halves[1], chunk(5), dev(dz=1), "b")]
+    state["b", 4] = [send(halves[0], chunk(4), dev(dz=3), "b")]
     own_g = [local(grad.at[:, pl.ds(h * HN, HN)], gg.at[h, y]) for h in range(2)]
     own_b = [local(basis_t, bt.at[pl.ds(0, KJ)])]
     own_plain = [local(mom_plain, mp), local(var_plain, vp)]
-    state["mv"] = [send(src.at[:, other], dst.at[c], dev(dc=1)) for src, dst in ((mom_rot, m2), (var_rot, v2))]
+    state["mv"] = [send(src.at[:, other], dst.at[c], dev(dc=1), "mv") for src, dst in ((mom_rot, m2), (var_rot, v2))]
     own_mv = [local(src.at[:, mine], dst.at[c]) for src, dst in ((mom_rot, m2), (var_rot, v2))]
 
-    norm[...] = jnp.zeros_like(norm)
+    norm[0] = jnp.zeros((2, 8, HN), F32)
     out_plain = []
 
     def done(copies):
@@ -147,7 +165,7 @@
                 m, v, d = adam(mp[s, lanes], vp[s, lanes], gg[h, y, s, :])
                 mp[s, lanes] = m
                 vp[s, lanes] = v
-                norm[0] += jnp.sum((d * d).reshape(8, 8, HN), axis=0)
+                norm[0, 0] += jnp.sum((d * d).reshape(8, 8, HN), axis=0)
 
         out_plain.append(local(mp, new_mom_plain))
         out_plain.append(local(vp, new_var_plain))
@@ -162,15 +180,15 @@
 
     def gf(h):
         arrived(("g", h, 1))
-        a = send(gg.at[h, ym, top], gg.at[h, ym, top], dev(dy=1))
+        slot = new_slot()
+        send(gg.at[h, ym, top], gg.at[h, ym, top], dev(dy=1), "g2", slot)
         arrived(("g", h, 3))
-        b = send(gg.at[h, yp, low], gg.at[h, yp, low], dev(dy=3))
-        state["g2", h] = [a, b]
+        send(gg.at[h, yp, low], gg.at[h, yp, low], dev(dy=3), "g2", slot)
+        state["g2", h] = [whole(gg.at[h, yo], slot)]
 
     def gs(h):
         done(own_g)
-        arrived(("g_rest", h, 1))
-        arrived(("g_rest", h, 3))
+        arrived(("g_rest", h))
         for n in (y, ym, yp):
             split_grad(h, n)
 
@@ -181,10 +199,10 @@
     def bf(way):
         if way == 0:
             arrived(("b", 3))
-            state["b", 6] = [send(chunk(3), chunk(6), dev(dz=1))]
+            state["b", 6] = [send(chunk(3), chunk(6), dev(dz=1), "bf")]
         else:
             arrived(("b", 2))
-            state["b", 7] = [send(chunk(2), chunk(7), dev(dz=3))]
+            state["b", 7] = [send(chunk(2), chunk(7), dev(dz=3), "bf")]
 
     def basis_there(lo, hi):
         for i in range(lo, hi):
@@ -227,7 +245,7 @@
                 part[h, n, lo + i] = new[i * QJ:(i + 1) * QJ, n * HN:(n + 1) * HN]
 
         group = pl.ds(lo, hi - lo)
-        state["x", g, h] = [send(part.at[h, :, group, other], rx.at[h, :, group], dev(dc=1))]
+        state["x", g, h] = [send(part.at[h, :, group, other], rx.at[h, :, group], dev(dc=1), "x")]
 
     def s1(g, h):
         lo, hi = GROUPS[g]
@@ -238,8 +256,8 @@
         (first, up), (second, dn) = ways(g)
         (first_r, up_r), (second_r, dn_r) = ways_share(g)
         state["ra", g, h] = [
-            send(part.at[h, xo, first, up], ra.at[h, 0, first_r, up_r], dev(dx=1)),
-            send(part.at[h, xo, second, dn], ra.at[h, 1, second_r, dn_r], dev(dx=3)),
+            send(part.at[h, xo, first, up], ra.at[h, 0, first_r, up_r], dev(dx=1), "ra"),
+            send(part.at[h, xo, second, dn], ra.at[h, 1, second_r, dn_r], dev(dx=3), "ra"),
         ]
 
     def s2(g, h):
@@ -250,11 +268,12 @@
         a, b = state.pop(("ra", g, h))
         a.wait_recv()
         part[h, xp, first, up, :] += ra[h, 0, first_r, up_r, :]
-        a = send(part.at[h, xp, group, mine], rb.at[h, 0, group], dev(dx=1))
+        slot = new_slot()
+        send(part.at[h, xp, group, mine], rb.at[h, 0, group], dev(dx=1), "rb", slot)
         b.wait_recv()
         part[h, xm, second, dn, :] += ra[h, 1, second_r, dn_r, :]
-        b = send(part.at[h, xm, group, mine], rb.at[h, 1, group], dev(dx=3))
-        state["rb", g, h] = [a, b]
+        send(part.at[h, xm, group, mine], rb.at[h, 1, group], dev(dx=3), "rb", slot)
+        state["rb", g, h] = [whole(rb.at[h, :, group], slot)]
 
     def s3(g, h):
         lo, hi = GROUPS[g]
@@ -262,12 +281,17 @@
         arrived(("rb", g, h))
         rt[h, group] = part[h, x, group, mine, :] + rb[h, 0, group] + rb[h, 1, group]
         for i in away(g):
-            state["at", i, h] = [send(rt.at[h, i], at.at[h, i], dev(dz=CHUNKS[i][0]))]
+            state["at", i, h] = [send(rt.at[h, i], at.at[h, i], dev(dz=CHUNKS[i][0]), "at")]
 
     def s4(g, h):
         arrived("mv")
         done(own_mv)
-        for i in range(*GROUPS[g]):
+        lo, hi = GROUPS[g]
+        if away(g):
+            assert away(g) == list(range(lo, hi))
+            slot = new_slot()
+            state["d", g, h] = [whole(dd.at[h, x, pl.ds(lo, hi - lo), mine], slot)]
+        for i in range(lo, hi):
             off, q = CHUNKS[i]
             arrived(("at", i, h))
             values = at[h, i] if off else rt[h, i]
@@ -279,33 +303,40 @@
             v2[half, q, :, lanes] = v
             if off:
                 direc[h, i] = d
-                state["d", i, h] = [send(direc.at[h, i], dd.at[h, x, i, mine], dev(dz=4 - off))]
+                send(direc.at[h, i], dd.at[h, x, i, mine], dev(dz=4 - off), "d", slot)
             else:
                 dd[h, x, i, mine, :] = d
 
     def s5(g, h):
         lo, hi = GROUPS[g]
-        for i in away(g):
-            arrived(("d", i, h))
+        arrived(("d", g, h))
         t = dd.at[h, x, pl.ds(lo, hi - lo), mine]
-        state["ag", g, h] = [send(t, t, dev(dx=1)), send(t, t, dev(dx=3))]
+        state["ag", g, h] = [send(t, t, dev(dx=1), "ag"), send(t, t, dev(dx=3), "ag")]
 
     def s6(g, h):
         (first, up), (second, dn) = ways(g)
         a, b = state.pop(("ag", g, h))
         a.wait_recv()
         t = dd.at[h, xm, first, up]
-        a = send(t, t, dev(dx=1))
+        slot = new_slot()
+        send(t, t, dev(dx=1), "ag2", slot)
         b.wait_recv()
         t = dd.at[h, xp, second, dn]
-        b = send(t, t, dev(dx=3))
-        state["ag2", g, h] = [a, b]
+        send(t, t, dev(dx=3), "ag2", slot)
+        lo, hi = GROUPS[g]
+        state["ag2", g, h] = [whole(dd.at[h, xo, pl.ds(lo, hi - lo), mine], slot)]
 
     def s7(g, h):
         lo, hi = GROUPS[g]
         arrived(("ag2", g, h))
         t = dd.at[h, :, pl.ds(lo, hi - lo), mine]
-        state["dc", g, h] = [send(t, t, dev(dc=1))]
+        early = hi <= 4
+        if ("dc", early, h) not in state:
+            slot = new_slot()
+            chunks = pl.ds(0, 4) if early else pl.ds(4, 4)
+            state["dc", early, h] = [whole(dd.at[h, :, chunks, other], slot)]
+            state["dc_slot", early, h] = slot
+        send(t, t, dev(dc=1), "dc", state["dc_slot", early, h])
 
     def turn(p):
         ends = (0, 3, 7, 10, 14)
@@ -338,9 +369,7 @@
             back[h, n, s, :] = back[h, n, s, :] + tile if part_of else tile
 
     def directions_there(h, lo, hi):
-        for g, (first, end) in enumerate(GROUPS):
-            if lo <= first and end <= hi:
-                arrived(("dc", g, h))
+        arrived(("dc", hi <= 4, h))
 
     def ya0(h):
         directions_there(h, 0, 4)
@@ -352,22 +381,26 @@
         directions_there(h, 4, 8)
         split_direction(h, 1)
         product_two(h, 1, top)
-        state["ya", h] = [send(back.at[h, yo, top], ya.at[h, 0], dev(dy=1))]
-        state["yb", h] = [send(back.at[h, ym, top], yb.at[h, 1, top], dev(dy=3))]
+        state["ya", h] = [send(back.at[h, yo, top], ya.at[h, 0], dev(dy=1), "ya")]
+        slot = new_slot()
+        state["yb_slot", h] = slot
+        state["yb", h] = [whole(yb.at[h], slot)]
+        send(back.at[h, ym, top], yb.at[h, 1, top], dev(dy=3), "yb", slot)
 
     def y0b(h):
         product_two(h, 1, low)
-        state["ya", h].append(send(back.at[h, yo, low], ya.at[h, 1], dev(dy=3)))
-        state["yb", h].append(send(back.at[h, yp, low], yb.at[h, 0, low], dev(dy=1)))
+        state["ya", h].append(send(back.at[h, yo, low], ya.at[h, 1], dev(dy=3), "ya"))
+        send(back.at[h, yp, low], yb.at[h, 0, low], dev(dy=1), "yb", state["yb_slot", h])
 
     def y1(h):
         up, dn = state.pop(("ya", h))
         up.wait_recv()
         back[h, yp, top, :] += ya[h, 0]
-        state["yb", h].append(send(back.at[h, yp, top], yb.at[h, 0, top], dev(dy=1)))
+        slot = state["yb_slot", h]
+        send(back.at[h, yp, top], yb.at[h, 0, top], dev(dy=1), "yb", slot)
         dn.wait_recv()
         back[h, ym, low, :] += ya[h, 1]
-        state["yb", h].append(send(back.at[h, ym, low], yb.at[h, 1, low], dev(dy=3)))
+        send(back.at[h, ym, low], yb.at[h, 1, low], dev(dy=3), "yb", slot)
 
     out_back_copies = []
 
@@ -379,7 +412,7 @@
             s = pl.ds(pl.multiple_of(i * 128, 128), 128)
             b = back[h, y, s, :] + yb[h, 0, s, :] + yb[h, 1, s, :]
             back[h, y, s, :] = b
-            norm[1] += jnp.sum((b * b).reshape(16, 8, HN), axis=0)
+            norm[0, 1] += jnp.sum((b * b).reshape(16, 8, HN), axis=0)
 
         out_back_copies.append(local(back.at[h, y], out_back.at[:, pl.ds(h * HN, HN)]))
 
@@ -406,27 +439,47 @@
             adams_left -= 1
             if adams_left == 0:
                 for src, dst in ((m2, new_mom_rot), (v2, new_var_rot)):
-                    out_rot.append(send(src.at[o], dst.at[:, mine], dev(dc=1)))
+                    out_rot.append(send(src.at[o], dst.at[:, mine], dev(dc=1), "out"))
                     out_rot_own.append(local(src.at[c], dst.at[:, mine]))
 
-    slot = 0
-    for moves in norm_moves:
-        copies = []
-        for to in moves:
-            copies.append((slot, send(norm, nrecv.at[slot], to)))
-            slot += 1
-        for _, copy in copies:
-            started.pop()
-            copy.wait()
-        total = norm[...]
-        for k, _ in copies:
-            total += nrecv[k]
-        norm[...] = total
-    last = local(norm, out_norm)
+    first = 0
+    for k, moves in enumerate(norm_moves):
+        slot = new_slot()
+        end = first + len(moves)
+        for i, to in enumerate(moves):
+            send(norm.at[k], nrecv.at[first + i], to, ("norm", k), slot)
+        whole(nrecv.at[pl.ds(first, len(moves))], slot).wait_recv()
+        total = norm[k]
+        for i in range(first, end):
+            total += nrecv[i]
+        norm[k + 1] = total
+        first = end
+    last = local(norm.at[len(norm_moves)], out_norm)
     assert count[0] <= N_COPIES and count[1] <= 16
 
-    for copy in started:
-        copy.wait_send()
+    share = rt
+    away_share = rt.at[:, pl.ds(2, 6)]
+    sent("g", gg.at[:, pl.ds(0, 2)])
+    sent("g2", gg.at[:, 0])
+    sent("b", bt.at[pl.ds(0, 2 * KJ)])
+    sent("bf", bt.at[pl.ds(0, KJ)])
+    sent("mv", m2.at[0], v2.at[0])
+    sent("x", rx)
+    sent("ra", share)
+    sent("rb", rb)
+    sent("at", away_share)
+    sent("d", away_share)
+    sent("ag", rb)
+    sent("ag2", share)
+    sent("dc", rx)
+    sent("ya", ya)
+    sent("yb", yb)
+    sent("out", m2.at[0], v2.at[0])
+    first = 0
+    for k, moves in enumerate(norm_moves):
+        sent(("norm", k), nrecv.at[pl.ds(first, len(moves))])
+        first += len(moves)
+    assert not sizes
     for copy in out_rot:
         copy.wait_recv()
     for copy in out_rot_own + out_plain + out_back_copies:
@@ -494,9 +547,9 @@
         pltpu.VMEM((2, 2, KI, HN), F32),
         pltpu.VMEM((KI, KN), F32),
         pltpu.VMEM((KI, KN), F32),
-        pltpu.VMEM((2, 8, HN), F32),
+        pltpu.VMEM((4, 2, 8, HN), F32),
         pltpu.VMEM((13, 2, 8, HN), F32),
-        pltpu.SemaphoreType.DMA((N_COPIES,)),
+        pltpu.SemaphoreType.DMA((24,)),
         pltpu.SemaphoreType.DMA((N_COPIES,)),
         pltpu.SemaphoreType.DMA((16,)),
     ]

time: 147 us -> 145 us (0.986)
  Pallas kernels: 146 us -> 144 us
    pallas_call x1, Pallas kernels: 142 us -> 140 us  [per_device(): pl.pallas_call(kernel, out_shape=(plain, norms, rot, rot, plain, plain),...]
where the time goes in v5:
time: 145 us
  Pallas kernels  144 us (99%)
    pallas_call x1, Pallas kernels, per_device(): pl.pallas_call(kernel, out_shape=(plain, norms, rot, rot, plain, plain),...  140 us
    pallas_call x1, Pallas kernels, per_device(): pl.pallas_call(finish, out_shape=(plain, rot, rot, plain, plain), in_spec...  4.12 us

profile of v5, /device:TPU:0, one launch (start us, length us, event | category | flops | bytes accessed | tf_op | source)
XLA Modules:
  0.0 144.8 jit_solution(1870910232675917585)
XLA Ops:
  0.6 139.9 %shard_map.101 = (f32[896,256]{1,0:T(8,128)}, f32[2,8,128]{2,1,0:T(8,128)}, f32[2,224,512]{2,1,0:T(8,128)}, f32[2,224,512]{2,1,0:T(8,128)}, f32[896,256]{1,0:T(8,128)}, /*index=5*/f32[896,256]{1,0:T(8,128)}) custom-call(f32[896,256]{1,0:T(8,128)} %grad.1, f32[448,896]{1,0:T(8,128)} %bitcast.5, f32[2,224,512]{2,1,0:T(8,128)} %bitcast.6, ...), custom_call_target="tpu_custom_call" | custom-call | flops 20000000000 | bytes 12000000 | tf_op jit(solution)/shard_map/pallas_call | solution.py:557
  140.5 4.1 %shard_map.102 = (f32[896,256]{1,0:T(8,128)}, f32[2,224,512]{2,1,0:T(8,128)}, f32[2,224,512]{2,1,0:T(8,128)}, f32[896,256]{1,0:T(8,128)}, f32[896,256]{1,0:T(8,128)}) custom-call(f32[896,256]{1,0:T(8,128)} %get-tuple-element.16.back, f32[2,8,128]{2,1,0:T(8,128)} %get-tuple-element.17.norm, f32[2,224,512]{2,1,0:T(8,128)} %get-tuple-element.18.refs_0_, ...), custom_call_target="tpu_custom_call" | custom-call | flops 1000000 | bytes 9000000 | tf_op jit(solution)/shard_map/pallas_call | solution.py:568

commit v6 on v5

--- a/solution.py
+++ b/solution.py
@@ -290,7 +290,7 @@
         if away(g):
             assert away(g) == list(range(lo, hi))
             slot = new_slot()
-            state["d", g, h] = [whole(dd.at[h, x, pl.ds(lo, hi - lo), mine], slot)]
+            state["d", g, h] = [whole(dd.at[h, 0, pl.ds(lo, hi - lo), mine], slot)]
         for i in range(lo, hi):
             off, q = CHUNKS[i]
             arrived(("at", i, h))
@@ -303,40 +303,46 @@
             v2[half, q, :, lanes] = v
             if off:
                 direc[h, i] = d
-                send(direc.at[h, i], dd.at[h, x, i, mine], dev(dz=4 - off), "d", slot)
+                send(direc.at[h, i], dd.at[h, 0, i, mine], dev(dz=4 - off), "d", slot)
             else:
-                dd[h, x, i, mine, :] = d
+                dd[h, 0, i, mine, :] = d
 
     def s5(g, h):
         lo, hi = GROUPS[g]
+        group = pl.ds(lo, hi - lo)
         arrived(("d", g, h))
-        t = dd.at[h, x, pl.ds(lo, hi - lo), mine]
-        state["ag", g, h] = [send(t, t, dev(dx=1), "ag"), send(t, t, dev(dx=3), "ag")]
-
-    def s6(g, h):
-        (first, up), (second, dn) = ways(g)
-        a, b = state.pop(("ag", g, h))
-        a.wait_recv()
-        t = dd.at[h, xm, first, up]
-        slot = new_slot()
-        send(t, t, dev(dx=1), "ag2", slot)
-        b.wait_recv()
-        t = dd.at[h, xp, second, dn]
-        send(t, t, dev(dx=3), "ag2", slot)
-        lo, hi = GROUPS[g]
-        state["ag2", g, h] = [whole(dd.at[h, xo, pl.ds(lo, hi - lo), mine], slot)]
-
-    def s7(g, h):
-        lo, hi = GROUPS[g]
-        arrived(("ag2", g, h))
-        t = dd.at[h, :, pl.ds(lo, hi - lo), mine]
+        t = dd.at[h, 0, group, mine]
+        state["ag", g, h] = [
+            send(t, dd.at[h, 2, group, mine], dev(dx=1), "ag"),
+            send(t, dd.at[h, 1, group, mine], dev(dx=3), "ag"),
+        ]
+
+    def to_other_core(g, h, first, blocks):
+        lo, hi = GROUPS[g]
         early = hi <= 4
         if ("dc", early, h) not in state:
             slot = new_slot()
             chunks = pl.ds(0, 4) if early else pl.ds(4, 4)
             state["dc", early, h] = [whole(dd.at[h, :, chunks, other], slot)]
             state["dc_slot", early, h] = slot
+        t = dd.at[h, pl.ds(first, blocks), pl.ds(lo, hi - lo), mine]
         send(t, t, dev(dc=1), "dc", state["dc_slot", early, h])
+
+    def s6(g, h):
+        lo, hi = GROUPS[g]
+        (first, up), (second, dn) = ways(g)
+        a, b = state.pop(("ag", g, h))
+        slot = new_slot()
+        a.wait_recv()
+        send(dd.at[h, 2, first, up], dd.at[h, 3, first, up], dev(dx=1), "ag2", slot)
+        b.wait_recv()
+        send(dd.at[h, 1, second, dn], dd.at[h, 3, second, dn], dev(dx=3), "ag2", slot)
+        state["ag2", g, h] = [whole(dd.at[h, 3, pl.ds(lo, hi - lo), mine], slot)]
+        to_other_core(g, h, 0, 3)
+
+    def s7(g, h):
+        arrived(("ag2", g, h))
+        to_other_core(g, h, 3, 1)
 
     def turn(p):
         ends = (0, 3, 7, 10, 14)
@@ -352,9 +358,12 @@
     def split_direction(h, part_of):
         @pl.loop(0, 4)
         def _(n):
+            d = (n + 4 - x) % 4
+            place = d + d // 2 * (1 - 2 * (d % 2))
+
             @pl.loop(0, 4)
             def _(i):
-                hi, lo = split(dd[h, n, part_of * 4 + i])
+                hi, lo = split(dd[h, place, part_of * 4 + i])
                 s = pl.ds(pl.multiple_of(i * QJ, QJ), QJ)
                 dhi[n, s, :] = hi
                 dlo[n, s, :] = lo
@@ -417,19 +426,19 @@
         out_back_copies.append(local(back.at[h, y], out_back.at[:, pl.ds(h * HN, HN)]))
 
     order = (
-        (turn, 0), (plain,), (gf, 0), (gs, 0), (gg_send, 1), (gs2, 0), (s0, 0, 0), (s0, 1, 0), (gf, 1),
-        (s1, 0, 0), (bf, 0), (turn, 1), (s2, 0, 0), (s1, 1, 0), (gs, 1), (bf, 1), (gs2, 1), (s0, 1, 1),
-        (s0, 0, 1), (s2, 1, 0), (s3, 0, 0), (s4, 0, 0), (s5, 0, 0), (s1, 1, 1), (s0, 2, 0), (s1, 0, 1),
-        (s0, 2, 1), (s2, 1, 1), (s1, 2, 0), (s2, 0, 1), (s3, 1, 0), (turn, 2), (s1, 2, 1), (s2, 2, 0),
-        (s6, 0, 0), (s3, 1, 1), (s0, 4, 0), (s2, 2, 1), (s0, 3, 0), (s0, 3, 1), (s1, 4, 0), (s3, 2, 0),
-        (s0, 4, 1), (s1, 3, 0), (s4, 1, 0), (s2, 4, 0), (s1, 3, 1), (s3, 2, 1), (s2, 3, 0), (s4, 2, 0),
-        (s1, 4, 1), (s5, 1, 0), (s3, 4, 0), (s3, 0, 1), (s2, 3, 1), (s3, 3, 0), (s7, 0, 0), (s5, 2, 0),
-        (s4, 4, 0), (turn, 3), (s6, 1, 0), (s4, 3, 0), (s3, 3, 1), (s2, 4, 1), (s4, 0, 1), (s4, 2, 1),
-        (s5, 4, 0), (s4, 1, 1), (s5, 3, 0), (s7, 1, 0), (s3, 4, 1), (s6, 2, 0), (s4, 3, 1), (s6, 4, 0),
-        (s6, 3, 0), (s5, 0, 1), (s5, 2, 1), (s7, 2, 0), (s5, 1, 1), (s7, 4, 0), (s4, 4, 1), (s7, 3, 0),
-        (ya0, 0), (s6, 0, 1), (s5, 4, 1), (y0, 0), (s6, 1, 1), (s7, 0, 1), (s5, 3, 1), (s6, 2, 1), (y0b, 0),
-        (s7, 1, 1), (s6, 4, 1), (s6, 3, 1), (s7, 2, 1), (s7, 4, 1), (y1, 0), (s7, 3, 1), (ya0, 1), (y0, 1),
-        (y0b, 1), (y1, 1), (y2, 0), (y2, 1),
+        (gf, 0), (gs, 0), (gg_send, 1), (gs2, 0), (s0, 0, 0), (s0, 1, 0), (turn, 0), (bf, 0), (s1, 0, 0),
+        (bf, 1), (gf, 1), (s2, 0, 0), (s1, 1, 0), (plain,), (s3, 0, 0), (gs, 1), (s4, 0, 0), (s5, 0, 0),
+        (gs2, 1), (s0, 0, 1), (s2, 1, 0), (s0, 1, 1), (s6, 0, 0), (s0, 2, 0), (s1, 0, 1), (s3, 1, 0),
+        (s1, 1, 1), (s2, 0, 1), (s0, 2, 1), (s2, 1, 1), (s1, 2, 0), (turn, 1), (s3, 0, 1), (s4, 0, 1),
+        (s5, 0, 1), (s1, 2, 1), (s3, 1, 1), (s7, 0, 0), (turn, 2), (s6, 0, 1), (s2, 2, 0), (s2, 2, 1),
+        (s0, 3, 0), (s0, 4, 0), (s4, 1, 0), (s0, 3, 1), (s1, 3, 0), (s3, 2, 0), (s1, 4, 0), (s5, 1, 0),
+        (s4, 1, 1), (s2, 3, 0), (s3, 2, 1), (s4, 2, 0), (s2, 4, 0), (s0, 4, 1), (s7, 0, 1), (s1, 3, 1),
+        (s3, 3, 0), (s6, 1, 0), (s3, 4, 0), (s1, 4, 1), (s2, 3, 1), (s7, 1, 0), (s5, 2, 0), (s4, 3, 0),
+        (s2, 4, 1), (s5, 1, 1), (s4, 4, 0), (s3, 3, 1), (ya0, 0), (s5, 4, 0), (s3, 4, 1), (s5, 3, 0),
+        (s6, 2, 0), (s4, 2, 1), (s4, 3, 1), (s6, 4, 0), (s4, 4, 1), (s6, 3, 0), (s5, 2, 1), (turn, 3),
+        (s7, 2, 0), (s7, 4, 0), (s7, 3, 0), (s5, 3, 1), (s6, 1, 1), (s5, 4, 1), (y0, 0), (s6, 3, 1),
+        (s7, 1, 1), (s6, 2, 1), (s6, 4, 1), (y0b, 0), (s7, 3, 1), (s7, 2, 1), (s7, 4, 1), (ya0, 1), (y0, 1),
+        (y0b, 1), (y1, 0), (y1, 1), (y2, 0), (y2, 1),
     )
     adams_left = 2 * len(GROUPS)
     out_rot, out_rot_own = [], []

time: 145 us -> 145 us (level)
  no operation moved by 1% of the time
where the time goes in v6:
time: 145 us
  Pallas kernels  144 us (99%)
    pallas_call x1, Pallas kernels, per_device(): pl.pallas_call(kernel, out_shape=(plain, norms, rot, rot, plain, plain),...  140 us
    pallas_call x1, Pallas kernels, per_device(): pl.pallas_call(finish, out_shape=(plain, rot, rot, plain, plain), in_spec...  4.12 us

profile of v6, /device:TPU:0, one launch (start us, length us, event | category | flops | bytes accessed | tf_op | source)
XLA Modules:
  0.0 145.2 jit_solution(4344183145257186295)
XLA Ops:
  0.6 140.3 %shard_map.101 = (f32[896,256]{1,0:T(8,128)}, f32[2,8,128]{2,1,0:T(8,128)}, f32[2,224,512]{2,1,0:T(8,128)}, f32[2,224,512]{2,1,0:T(8,128)}, f32[896,256]{1,0:T(8,128)}, /*index=5*/f32[896,256]{1,0:T(8,128)}) custom-call(f32[896,256]{1,0:T(8,128)} %grad.1, f32[448,896]{1,0:T(8,128)} %bitcast.5, f32[2,224,512]{2,1,0:T(8,128)} %bitcast.6, ...), custom_call_target="tpu_custom_call" | custom-call | flops 20000000000 | bytes 12000000 | tf_op jit(solution)/shard_map/pallas_call | solution.py:566
  140.9 4.1 %shard_map.102 = (f32[896,256]{1,0:T(8,128)}, f32[2,224,512]{2,1,0:T(8,128)}, f32[2,224,512]{2,1,0:T(8,128)}, f32[896,256]{1,0:T(8,128)}, f32[896,256]{1,0:T(8,128)}) custom-call(f32[896,256]{1,0:T(8,128)} %get-tuple-element.16.back, f32[2,8,128]{2,1,0:T(8,128)} %get-tuple-element.17.norm, f32[2,224,512]{2,1,0:T(8,128)} %get-tuple-element.18.refs_0_, ...), custom_call_target="tpu_custom_call" | custom-call | flops 1000000 | bytes 9000000 | tf_op jit(solution)/shard_map/pallas_call | solution.py:577

commit v7 on v5

--- a/solution.py
+++ b/solution.py
@@ -23,6 +23,7 @@
 CJ = QJ // 2
 CHUNKS = ((0, 0), (0, 1), (1, 1), (3, 0), (1, 0), (3, 1), (2, 0), (2, 1))
 GROUPS = ((0, 2), (2, 4), (4, 6), (6, 7), (7, 8))
+PRODUCTS = ((0, 1), (2,), (3, 4))
 N_COPIES = 128
 
 
@@ -230,22 +231,25 @@
         return [(pl.ds(lo, 1), pl.ds(0, CJ // 2)), (pl.ds(lo, 1), pl.ds(CJ // 2, CJ // 2))]
 
     def s0(g, h):
-        lo, hi = GROUPS[g]
+        if ("x", g, h) in state:
+            return
+        groups = next(p for p in PRODUCTS if g in p)
+        lo, hi = GROUPS[groups[0]][0], GROUPS[groups[-1]][1]
         basis_there(lo, hi)
         size = (hi - lo) * QJ
         high, rest = split(bt[lo * QJ:hi * QJ, :])
         lhi[:size, :] = high
         llo[:size, :] = rest
-
         rh = jnp.concatenate([ghi[h, n] for n in range(4)], axis=1)
         rl = jnp.concatenate([glo[h, n] for n in range(4)], axis=1)
         new = dot3(lhi[:size, :], llo[:size, :], rh, rl)
         for n in range(4):
             for i in range(hi - lo):
                 part[h, n, lo + i] = new[i * QJ:(i + 1) * QJ, n * HN:(n + 1) * HN]
-
-        group = pl.ds(lo, hi - lo)
-        state["x", g, h] = [send(part.at[h, :, group, other], rx.at[h, :, group], dev(dc=1), "x")]
+        for k in groups:
+            first, end = GROUPS[k]
+            group = pl.ds(first, end - first)
+            state["x", k, h] = [send(part.at[h, :, group, other], rx.at[h, :, group], dev(dc=1), "x")]
 
     def s1(g, h):
         lo, hi = GROUPS[g]
@@ -255,22 +259,20 @@
             part[h, n, group, mine, :] += rx[h, n, group]
         (first, up), (second, dn) = ways(g)
         (first_r, up_r), (second_r, dn_r) = ways_share(g)
-        state["ra", g, h] = [
-            send(part.at[h, xo, first, up], ra.at[h, 0, first_r, up_r], dev(dx=1), "ra"),
-            send(part.at[h, xo, second, dn], ra.at[h, 1, second_r, dn_r], dev(dx=3), "ra"),
-        ]
+        slot = new_slot()
+        state["ra", g, h] = [whole(rt.at[h, pl.ds(lo, hi - lo)], slot)]
+        send(part.at[h, xo, first, up], ra.at[h, 0, first_r, up_r], dev(dx=1), "ra", slot)
+        send(part.at[h, xo, second, dn], ra.at[h, 1, second_r, dn_r], dev(dx=3), "ra", slot)
 
     def s2(g, h):
         lo, hi = GROUPS[g]
         group = pl.ds(lo, hi - lo)
         (first, up), (second, dn) = ways(g)
         (first_r, up_r), (second_r, dn_r) = ways_share(g)
-        a, b = state.pop(("ra", g, h))
-        a.wait_recv()
+        arrived(("ra", g, h))
         part[h, xp, first, up, :] += ra[h, 0, first_r, up_r, :]
         slot = new_slot()
         send(part.at[h, xp, group, mine], rb.at[h, 0, group], dev(dx=1), "rb", slot)
-        b.wait_recv()
         part[h, xm, second, dn, :] += ra[h, 1, second_r, dn_r, :]
         send(part.at[h, xm, group, mine], rb.at[h, 1, group], dev(dx=3), "rb", slot)
         state["rb", g, h] = [whole(rb.at[h, :, group], slot)]
@@ -311,16 +313,17 @@
         lo, hi = GROUPS[g]
         arrived(("d", g, h))
         t = dd.at[h, x, pl.ds(lo, hi - lo), mine]
-        state["ag", g, h] = [send(t, t, dev(dx=1), "ag"), send(t, t, dev(dx=3), "ag")]
+        slot = new_slot()
+        send(t, t, dev(dx=1), "ag", slot)
+        send(t, t, dev(dx=3), "ag", slot)
+        state["ag", g, h] = [whole(rb.at[h, :, pl.ds(lo, hi - lo)], slot)]
 
     def s6(g, h):
         (first, up), (second, dn) = ways(g)
-        a, b = state.pop(("ag", g, h))
-        a.wait_recv()
+        arrived(("ag", g, h))
         t = dd.at[h, xm, first, up]
         slot = new_slot()
         send(t, t, dev(dx=1), "ag2", slot)
-        b.wait_recv()
         t = dd.at[h, xp, second, dn]
         send(t, t, dev(dx=3), "ag2", slot)
         lo, hi = GROUPS[g]
@@ -374,8 +377,7 @@
     def ya0(h):
         directions_there(h, 0, 4)
         split_direction(h, 0)
-        product_two(h, 0, top)
-        product_two(h, 0, low)
+        product_two(h, 0, pl.ds(0, KI))
 
     def y0(h):
         directions_there(h, 4, 8)
@@ -526,8 +528,8 @@
         pltpu.VMEM((2, 4, KI, HN), BF16),
         pltpu.VMEM((2, 4, KI, HN), BF16),
         pltpu.VMEM((4 * KJ, KI), F32),
-        pltpu.VMEM((KJ, KI), BF16),
-        pltpu.VMEM((KJ, KI), BF16),
+        pltpu.VMEM((2 * KJ, KI), BF16),
+        pltpu.VMEM((2 * KJ, KI), BF16),
         pltpu.VMEM((KI, 4 * KJ), BF16),
         pltpu.VMEM((KI, 4 * KJ), BF16),
         pltpu.VMEM((2, 4, 8, QJ, HN), F32),

time: 145 us -> 145 us (level)
  no operation moved by 1% of the time
where the time goes in v7:
time: 145 us
  Pallas kernels  144 us (99%)
    pallas_call x1, Pallas kernels, per_device(): pl.pallas_call(kernel, out_shape=(plain, norms, rot, rot, plain, plain),...  140 us
    pallas_call x1, Pallas kernels, per_device(): pl.pallas_call(finish, out_shape=(plain, rot, rot, plain, plain), in_spec...  4.12 us

profile of v7, /device:TPU:0, one launch (start us, length us, event | category | flops | bytes accessed | tf_op | source)
XLA Modules:
  0.0 144.6 jit_solution(10853558005150006594)
XLA Ops:
  0.6 139.7 %shard_map.101 = (f32[896,256]{1,0:T(8,128)}, f32[2,8,128]{2,1,0:T(8,128)}, f32[2,224,512]{2,1,0:T(8,128)}, f32[2,224,512]{2,1,0:T(8,128)}, f32[896,256]{1,0:T(8,128)}, /*index=5*/f32[896,256]{1,0:T(8,128)}) custom-call(f32[896,256]{1,0:T(8,128)} %grad.1, f32[448,896]{1,0:T(8,128)} %bitcast.5, f32[2,224,512]{2,1,0:T(8,128)} %bitcast.6, ...), custom_call_target="tpu_custom_call" | custom-call | flops 20000000000 | bytes 12000000 | tf_op jit(solution)/shard_map/pallas_call | solution.py:559
  140.3 4.1 %shard_map.102 = (f32[896,256]{1,0:T(8,128)}, f32[2,224,512]{2,1,0:T(8,128)}, f32[2,224,512]{2,1,0:T(8,128)}, f32[896,256]{1,0:T(8,128)}, f32[896,256]{1,0:T(8,128)}) custom-call(f32[896,256]{1,0:T(8,128)} %get-tuple-element.16.back, f32[2,8,128]{2,1,0:T(8,128)} %get-tuple-element.17.norm, f32[2,224,512]{2,1,0:T(8,128)} %get-tuple-element.18.refs_0_, ...), custom_call_target="tpu_custom_call" | custom-call | flops 1000000 | bytes 9000000 | tf_op jit(solution)/shard_map/pallas_call | solution.py:570

commit v8 on v6

--- a/solution.py
+++ b/solution.py
@@ -23,6 +23,7 @@
 CJ = QJ // 2
 CHUNKS = ((0, 0), (0, 1), (1, 1), (3, 0), (1, 0), (3, 1), (2, 0), (2, 1))
 GROUPS = ((0, 2), (2, 4), (4, 6), (6, 7), (7, 8))
+PRODUCTS = ((0,), (1,), (2,), (3, 4))
 N_COPIES = 128
 
 
@@ -63,7 +64,6 @@
         q = (y + dy) % 4 * 4 + (z + dz) % 4
         return (r, q)
 
-    xp, xm, xo = (x + 1) % 4, (x + 3) % 4, (x + 2) % 4
     yp, ym, yo = (y + 1) % 4, (y + 3) % 4, (y + 2) % 4
     mine = pl.ds(pl.multiple_of(c * CJ, CJ), CJ)
     other = pl.ds(pl.multiple_of(o * CJ, CJ), CJ)
@@ -229,57 +229,66 @@
             return [(pl.ds(lo, 1), pl.ds(0, CJ)), (pl.ds(lo + 1, 1), pl.ds(0, CJ))]
         return [(pl.ds(lo, 1), pl.ds(0, CJ // 2)), (pl.ds(lo, 1), pl.ds(CJ // 2, CJ // 2))]
 
+    def place(n):
+        d = (n + 4 - x) % 4
+        return d + d // 2 * (1 - 2 * (d % 2))
+
     def s0(g, h):
-        lo, hi = GROUPS[g]
+        if ("x", g, h) in state:
+            return
+        groups = next(p for p in PRODUCTS if g in p)
+        lo, hi = GROUPS[groups[0]][0], GROUPS[groups[-1]][1]
         basis_there(lo, hi)
         size = (hi - lo) * QJ
         high, rest = split(bt[lo * QJ:hi * QJ, :])
         lhi[:size, :] = high
         llo[:size, :] = rest
-
         rh = jnp.concatenate([ghi[h, n] for n in range(4)], axis=1)
         rl = jnp.concatenate([glo[h, n] for n in range(4)], axis=1)
         new = dot3(lhi[:size, :], llo[:size, :], rh, rl)
         for n in range(4):
             for i in range(hi - lo):
-                part[h, n, lo + i] = new[i * QJ:(i + 1) * QJ, n * HN:(n + 1) * HN]
-
+                part[h, place(n), lo + i] = new[i * QJ:(i + 1) * QJ, n * HN:(n + 1) * HN]
+        for k in groups:
+            first, end = GROUPS[k]
+            group = pl.ds(first, end - first)
+            state["xo", k, h] = [send(part.at[h, 3, group, other], rx.at[h, 3, group], dev(dc=1), "x")]
+            near = pl.ds(0, 3)
+            state["x", k, h] = [send(part.at[h, near, group, other], rx.at[h, near, group], dev(dc=1), "x")]
+
+    def s1(g, h):
+        lo, hi = GROUPS[g]
+        arrived(("xo", g, h))
         group = pl.ds(lo, hi - lo)
-        state["x", g, h] = [send(part.at[h, :, group, other], rx.at[h, :, group], dev(dc=1), "x")]
-
-    def s1(g, h):
-        lo, hi = GROUPS[g]
-        arrived(("x", g, h))
-        group = pl.ds(lo, hi - lo)
-        for n in range(4):
-            part[h, n, group, mine, :] += rx[h, n, group]
+        part[h, 3, group, mine, :] += rx[h, 3, group]
         (first, up), (second, dn) = ways(g)
         (first_r, up_r), (second_r, dn_r) = ways_share(g)
-        state["ra", g, h] = [
-            send(part.at[h, xo, first, up], ra.at[h, 0, first_r, up_r], dev(dx=1), "ra"),
-            send(part.at[h, xo, second, dn], ra.at[h, 1, second_r, dn_r], dev(dx=3), "ra"),
-        ]
+        slot = new_slot()
+        state["ra", g, h] = [whole(rt.at[h, pl.ds(lo, hi - lo)], slot)]
+        send(part.at[h, 3, first, up], ra.at[h, 0, first_r, up_r], dev(dx=1), "ra", slot)
+        send(part.at[h, 3, second, dn], ra.at[h, 1, second_r, dn_r], dev(dx=3), "ra", slot)
 
     def s2(g, h):
         lo, hi = GROUPS[g]
         group = pl.ds(lo, hi - lo)
         (first, up), (second, dn) = ways(g)
         (first_r, up_r), (second_r, dn_r) = ways_share(g)
-        a, b = state.pop(("ra", g, h))
-        a.wait_recv()
-        part[h, xp, first, up, :] += ra[h, 0, first_r, up_r, :]
+        arrived(("x", g, h))
+        for n in range(3):
+            part[h, n, group, mine, :] += rx[h, n, group]
+        arrived(("ra", g, h))
+        part[h, 1, first, up, :] += ra[h, 0, first_r, up_r, :]
         slot = new_slot()
-        send(part.at[h, xp, group, mine], rb.at[h, 0, group], dev(dx=1), "rb", slot)
-        b.wait_recv()
-        part[h, xm, second, dn, :] += ra[h, 1, second_r, dn_r, :]
-        send(part.at[h, xm, group, mine], rb.at[h, 1, group], dev(dx=3), "rb", slot)
+        send(part.at[h, 1, group, mine], rb.at[h, 0, group], dev(dx=1), "rb", slot)
+        part[h, 2, second, dn, :] += ra[h, 1, second_r, dn_r, :]
+        send(part.at[h, 2, group, mine], rb.at[h, 1, group], dev(dx=3), "rb", slot)
         state["rb", g, h] = [whole(rb.at[h, :, group], slot)]
 
     def s3(g, h):
         lo, hi = GROUPS[g]
         group = pl.ds(lo, hi - lo)
         arrived(("rb", g, h))
-        rt[h, group] = part[h, x, group, mine, :] + rb[h, 0, group] + rb[h, 1, group]
+        rt[h, group] = part[h, 0, group, mine, :] + rb[h, 0, group] + rb[h, 1, group]
         for i in away(g):
             state["at", i, h] = [send(rt.at[h, i], at.at[h, i], dev(dz=CHUNKS[i][0]), "at")]
 
@@ -312,10 +321,10 @@
         group = pl.ds(lo, hi - lo)
         arrived(("d", g, h))
         t = dd.at[h, 0, group, mine]
-        state["ag", g, h] = [
-            send(t, dd.at[h, 2, group, mine], dev(dx=1), "ag"),
-            send(t, dd.at[h, 1, group, mine], dev(dx=3), "ag"),
-        ]
+        slot = new_slot()
+        send(t, dd.at[h, 2, group, mine], dev(dx=1), "ag", slot)
+        send(t, dd.at[h, 1, group, mine], dev(dx=3), "ag", slot)
+        state["ag", g, h] = [whole(dd.at[h, pl.ds(1, 2), group, mine], slot)]
 
     def to_other_core(g, h, first, blocks):
         lo, hi = GROUPS[g]
@@ -331,11 +340,9 @@
     def s6(g, h):
         lo, hi = GROUPS[g]
         (first, up), (second, dn) = ways(g)
-        a, b = state.pop(("ag", g, h))
+        arrived(("ag", g, h))
         slot = new_slot()
-        a.wait_recv()
         send(dd.at[h, 2, first, up], dd.at[h, 3, first, up], dev(dx=1), "ag2", slot)
-        b.wait_recv()
         send(dd.at[h, 1, second, dn], dd.at[h, 3, second, dn], dev(dx=3), "ag2", slot)
         state["ag2", g, h] = [whole(dd.at[h, 3, pl.ds(lo, hi - lo), mine], slot)]
         to_other_core(g, h, 0, 3)
@@ -358,12 +365,11 @@
     def split_direction(h, part_of):
         @pl.loop(0, 4)
         def _(n):
-            d = (n + 4 - x) % 4
-            place = d + d // 2 * (1 - 2 * (d % 2))
+            here = place(n)
 
             @pl.loop(0, 4)
             def _(i):
-                hi, lo = split(dd[h, place, part_of * 4 + i])
+                hi, lo = split(dd[h, here, part_of * 4 + i])
                 s = pl.ds(pl.multiple_of(i * QJ, QJ), QJ)
                 dhi[n, s, :] = hi
                 dlo[n, s, :] = lo
@@ -383,8 +389,7 @@
     def ya0(h):
         directions_there(h, 0, 4)
         split_direction(h, 0)
-        product_two(h, 0, top)
-        product_two(h, 0, low)
+        product_two(h, 0, pl.ds(0, KI))
 
     def y0(h):
         directions_there(h, 4, 8)
@@ -426,19 +431,19 @@
         out_back_copies.append(local(back.at[h, y], out_back.at[:, pl.ds(h * HN, HN)]))
 
     order = (
-        (gf, 0), (gs, 0), (gg_send, 1), (gs2, 0), (s0, 0, 0), (s0, 1, 0), (turn, 0), (bf, 0), (s1, 0, 0),
-        (bf, 1), (gf, 1), (s2, 0, 0), (s1, 1, 0), (plain,), (s3, 0, 0), (gs, 1), (s4, 0, 0), (s5, 0, 0),
-        (gs2, 1), (s0, 0, 1), (s2, 1, 0), (s0, 1, 1), (s6, 0, 0), (s0, 2, 0), (s1, 0, 1), (s3, 1, 0),
-        (s1, 1, 1), (s2, 0, 1), (s0, 2, 1), (s2, 1, 1), (s1, 2, 0), (turn, 1), (s3, 0, 1), (s4, 0, 1),
-        (s5, 0, 1), (s1, 2, 1), (s3, 1, 1), (s7, 0, 0), (turn, 2), (s6, 0, 1), (s2, 2, 0), (s2, 2, 1),
-        (s0, 3, 0), (s0, 4, 0), (s4, 1, 0), (s0, 3, 1), (s1, 3, 0), (s3, 2, 0), (s1, 4, 0), (s5, 1, 0),
-        (s4, 1, 1), (s2, 3, 0), (s3, 2, 1), (s4, 2, 0), (s2, 4, 0), (s0, 4, 1), (s7, 0, 1), (s1, 3, 1),
-        (s3, 3, 0), (s6, 1, 0), (s3, 4, 0), (s1, 4, 1), (s2, 3, 1), (s7, 1, 0), (s5, 2, 0), (s4, 3, 0),
-        (s2, 4, 1), (s5, 1, 1), (s4, 4, 0), (s3, 3, 1), (ya0, 0), (s5, 4, 0), (s3, 4, 1), (s5, 3, 0),
-        (s6, 2, 0), (s4, 2, 1), (s4, 3, 1), (s6, 4, 0), (s4, 4, 1), (s6, 3, 0), (s5, 2, 1), (turn, 3),
-        (s7, 2, 0), (s7, 4, 0), (s7, 3, 0), (s5, 3, 1), (s6, 1, 1), (s5, 4, 1), (y0, 0), (s6, 3, 1),
-        (s7, 1, 1), (s6, 2, 1), (s6, 4, 1), (y0b, 0), (s7, 3, 1), (s7, 2, 1), (s7, 4, 1), (ya0, 1), (y0, 1),
-        (y0b, 1), (y1, 0), (y1, 1), (y2, 0), (y2, 1),
+        (gf, 0), (turn, 0), (gg_send, 1), (gs, 0), (gs2, 0), (s0, 0, 0), (bf, 1), (s1, 0, 0), (gf, 1),
+        (s2, 0, 0), (turn, 1), (s0, 1, 0), (s3, 0, 0), (s1, 1, 0), (gs, 1), (s4, 0, 0), (s5, 0, 0), (gs2, 1),
+        (s0, 0, 1), (s2, 1, 0), (bf, 0), (s0, 1, 1), (s1, 0, 1), (s0, 2, 0), (s6, 0, 0), (s1, 1, 1),
+        (s2, 0, 1), (s1, 2, 0), (s2, 1, 1), (s0, 2, 1), (turn, 2), (s3, 0, 1), (s3, 1, 0), (s1, 2, 1),
+        (s7, 0, 0), (s2, 2, 0), (s4, 0, 1), (s5, 0, 1), (s3, 1, 1), (s2, 2, 1), (s3, 2, 0), (s0, 3, 0),
+        (s0, 4, 0), (s1, 3, 0), (s4, 1, 0), (s3, 2, 1), (s1, 4, 0), (s2, 3, 0), (s4, 2, 0), (s2, 4, 0),
+        (s5, 1, 0), (s3, 3, 0), (s0, 4, 1), (s5, 2, 0), (s3, 4, 0), (s0, 3, 1), (s4, 3, 0), (turn, 3),
+        (s6, 1, 0), (s1, 4, 1), (s4, 4, 0), (s4, 1, 1), (s4, 2, 1), (s5, 3, 0), (s1, 3, 1), (s7, 1, 0),
+        (s2, 4, 1), (s5, 4, 0), (s6, 2, 0), (s6, 3, 0), (ya0, 0), (s6, 4, 0), (s2, 3, 1), (s7, 2, 0),
+        (s3, 4, 1), (s5, 1, 1), (s7, 3, 0), (s7, 4, 0), (s6, 0, 1), (s3, 3, 1), (y0, 0), (s6, 1, 1),
+        (s4, 4, 1), (s4, 3, 1), (s5, 2, 1), (y0b, 0), (s7, 1, 1), (s7, 0, 1), (s5, 4, 1), (s6, 2, 1),
+        (s5, 3, 1), (ya0, 1), (s7, 2, 1), (s6, 3, 1), (s6, 4, 1), (y1, 0), (s7, 3, 1), (s7, 4, 1), (y0, 1),
+        (y2, 0), (y0b, 1), (y1, 1), (plain,), (y2, 1),
     )
     adams_left = 2 * len(GROUPS)
     out_rot, out_rot_own = [], []
@@ -535,8 +540,8 @@
         pltpu.VMEM((2, 4, KI, HN), BF16),
         pltpu.VMEM((2, 4, KI, HN), BF16),
         pltpu.VMEM((4 * KJ, KI), F32),
-        pltpu.VMEM((KJ, KI), BF16),
-        pltpu.VMEM((KJ, KI), BF16),
+        pltpu.VMEM((2 * KJ, KI), BF16),
+        pltpu.VMEM((2 * KJ, KI), BF16),
         pltpu.VMEM((KI, 4 * KJ), BF16),
         pltpu.VMEM((KI, 4 * KJ), BF16),
         pltpu.VMEM((2, 4, 8, QJ, HN), F32),

time: 145 us -> 147 us (1.014)
  Pallas kernels: 144 us -> 146 us
    pallas_call x1, Pallas kernels: 140 us -> 142 us  [per_device(): pl.pallas_call(kernel, out_shape=(plain, norms, rot, rot, plain, plain),...]
where the time goes in v8:
time: 147 us
  Pallas kernels  146 us (99%)
    pallas_call x1, Pallas kernels, per_device(): pl.pallas_call(kernel, out_shape=(plain, norms, rot, rot, plain, plain),...  142 us
    pallas_call x1, Pallas kernels, per_device(): pl.pallas_call(finish, out_shape=(plain, rot, rot, plain, plain), in_spec...  4.12 us

profile of v8, /device:TPU:0, one launch (start us, length us, event | category | flops | bytes accessed | tf_op | source)
XLA Modules:
  0.0 147.2 jit_solution(15948703318485288210)
XLA Ops:
  0.6 142.3 %shard_map.101 = (f32[896,256]{1,0:T(8,128)}, f32[2,8,128]{2,1,0:T(8,128)}, f32[2,224,512]{2,1,0:T(8,128)}, f32[2,224,512]{2,1,0:T(8,128)}, f32[896,256]{1,0:T(8,128)}, /*index=5*/f32[896,256]{1,0:T(8,128)}) custom-call(f32[896,256]{1,0:T(8,128)} %grad.1, f32[448,896]{1,0:T(8,128)} %bitcast.5, f32[2,224,512]{2,1,0:T(8,128)} %bitcast.6, ...), custom_call_target="tpu_custom_call" | custom-call | flops 20000000000 | bytes 12000000 | tf_op jit(solution)/shard_map/pallas_call | solution.py:571
  143.0 4.1 %shard_map.102 = (f32[896,256]{1,0:T(8,128)}, f32[2,224,512]{2,1,0:T(8,128)}, f32[2,224,512]{2,1,0:T(8,128)}, f32[896,256]{1,0:T(8,128)}, f32[896,256]{1,0:T(8,128)}) custom-call(f32[896,256]{1,0:T(8,128)} %get-tuple-element.16.back, f32[2,8,128]{2,1,0:T(8,128)} %get-tuple-element.17.norm, f32[2,224,512]{2,1,0:T(8,128)} %get-tuple-element.18.refs_0_, ...), custom_call_target="tpu_custom_call" | custom-call | flops 1000000 | bytes 9000000 | tf_op jit(solution)/shard_map/pallas_call | solution.py:582

commit v9 on v7

--- a/solution.py
+++ b/solution.py
@@ -23,7 +23,7 @@
 CJ = QJ // 2
 CHUNKS = ((0, 0), (0, 1), (1, 1), (3, 0), (1, 0), (3, 1), (2, 0), (2, 1))
 GROUPS = ((0, 2), (2, 4), (4, 6), (6, 7), (7, 8))
-PRODUCTS = ((0, 1), (2,), (3, 4))
+PRODUCTS = ((0,), (1,), (2,), (3, 4))
 N_COPIES = 128
 
 
@@ -377,7 +377,8 @@
     def ya0(h):
         directions_there(h, 0, 4)
         split_direction(h, 0)
-        product_two(h, 0, pl.ds(0, KI))
+        product_two(h, 0, top)
+        product_two(h, 0, low)
 
     def y0(h):
         directions_there(h, 4, 8)

time: 145 us -> 145 us (level)
  no operation moved by 1% of the time
where the time goes in v9:
time: 145 us
  Pallas kernels  144 us (99%)
    pallas_call x1, Pallas kernels, per_device(): pl.pallas_call(kernel, out_shape=(plain, norms, rot, rot, plain, plain),...  140 us
    pallas_call x1, Pallas kernels, per_device(): pl.pallas_call(finish, out_shape=(plain, rot, rot, plain, plain), in_spec...  4.12 us

profile of v9, /device:TPU:0, one launch (start us, length us, event | category | flops | bytes accessed | tf_op | source)
XLA Modules:
  0.0 144.7 jit_solution(3362775639623461154)
XLA Ops:
  0.6 139.7 %shard_map.101 = (f32[896,256]{1,0:T(8,128)}, f32[2,8,128]{2,1,0:T(8,128)}, f32[2,224,512]{2,1,0:T(8,128)}, f32[2,224,512]{2,1,0:T(8,128)}, f32[896,256]{1,0:T(8,128)}, /*index=5*/f32[896,256]{1,0:T(8,128)}) custom-call(f32[896,256]{1,0:T(8,128)} %grad.1, f32[448,896]{1,0:T(8,128)} %bitcast.5, f32[2,224,512]{2,1,0:T(8,128)} %bitcast.6, ...), custom_call_target="tpu_custom_call" | custom-call | flops 20000000000 | bytes 12000000 | tf_op jit(solution)/shard_map/pallas_call | solution.py:560
  140.4 4.1 %shard_map.102 = (f32[896,256]{1,0:T(8,128)}, f32[2,224,512]{2,1,0:T(8,128)}, f32[2,224,512]{2,1,0:T(8,128)}, f32[896,256]{1,0:T(8,128)}, f32[896,256]{1,0:T(8,128)}) custom-call(f32[896,256]{1,0:T(8,128)} %get-tuple-element.16.back, f32[2,8,128]{2,1,0:T(8,128)} %get-tuple-element.17.norm, f32[2,224,512]{2,1,0:T(8,128)} %get-tuple-element.18.refs_0_, ...), custom_call_target="tpu_custom_call" | custom-call | flops 1000000 | bytes 9000000 | tf_op jit(solution)/shard_map/pallas_call | solution.py:571
